TPU v7x, 256 devices: a whole 4x4x8 slice. The times are simulated.
256 devices in a mesh: dp: 16 (over y_lo, x, core), tensor: 16 (over y_hi, z).
Axes of the slice: x: 4, y: 4 (y_hi: 2, y_lo: 2; y = y_hi * 2 + y_lo), z: 8, core: 2. Of those that a mesh axis runs over, the one named last changes fastest.
Arguments:
- sublayer_input: bfloat16 [4096, 6144], P('dp'), may hold values from -6 to 6
- w_qkv: bfloat16 [6144, 32, 384], P('dp', 'tensor'), may hold values from -0.078125 to 0.078125
- w_out: bfloat16 [6144, 32, 128], P('dp', 'tensor'), may hold values from -0.5 to 0.5
- upstream_grad: bfloat16 [4096, 6144], P('dp'), may hold values from -6 to 6
Outputs:
- hidden_input_gradient: bfloat16 [4096, 6144], P(('dp', 'tensor'))
- grad_qkv: float32 [6144, 32, 384], P('dp', 'tensor')
- grad_out: float32 [6144, 32, 128], P('dp', 'tensor')
All inputs are finite; a program needn't handle non-finite values.
Results may differ from a plain program's by a relative error of at most 0.023.
Values may be sent and summed in bfloat16 or wider, within the bound.
A program may use at most 128 MiB of HBM per device.

v0:
```python
import math

import jax
import jax.numpy as jnp
from jax import lax
from jax.sharding import PartitionSpec as P

EPS = 1e-05


def apply_layer_norm(hidden_rows):
    hidden_rows = hidden_rows.astype(jnp.float32)
    centered = hidden_rows - jnp.mean(hidden_rows, axis=-1, keepdims=True)
    inverse_deviation = lax.rsqrt(jnp.mean(centered * centered, axis=-1, keepdims=True) + EPS)
    return (centered * inverse_deviation, inverse_deviation)


def rows_product(left_rows, right_rows):
    return lax.dot_general(
        left_rows, right_rows, (((0,), (0,)), ((), ())), preferred_element_type=jnp.float32
    )


def per_device(sublayer_input, w_qkv, w_out, upstream_grad):
    n_data = lax.axis_size("dp")
    n_tensor = lax.axis_size("tensor")
    seq_len = sublayer_input.shape[0]
    model_width = sublayer_input.shape[1]
    row_block_span = seq_len // n_tensor
    piece_rows = w_qkv.shape[0]
    head_count = w_qkv.shape[1]
    head_width = w_out.shape[2]
    qkv_width = head_count * 3 * head_width
    score_scale = 1.0 / math.sqrt(head_width)
    standardized_input, inverse_deviation = apply_layer_norm(sublayer_input)
    normalized_full_rows = standardized_input.astype(jnp.bfloat16)
    qkv_whole, out_whole = (
        lax.all_gather(w_qkv, "dp", axis=0, tiled=True),
        lax.all_gather(w_out, "dp", axis=0, tiled=True),
    )
    qkv_whole = qkv_whole.reshape(model_width, qkv_width)
    out_whole = out_whole.reshape(model_width, head_count * head_width)
    projected = jnp.dot(normalized_full_rows, qkv_whole, preferred_element_type=jnp.float32)
    context_term = jnp.dot(upstream_grad, out_whole, preferred_element_type=jnp.float32)
    qkv = projected.astype(jnp.bfloat16).reshape(seq_len, head_count, 3 * head_width)
    queries = qkv[..., :head_width]
    key_part = qkv[..., head_width : 2 * head_width]
    value_part = qkv[..., 2 * head_width :]
    scores = (
        jnp.einsum("qhe,khe->hqk", queries, key_part, preferred_element_type=jnp.float32)
        * score_scale
    )
    raised = jnp.exp(scores)
    attn_probs = raised / jnp.sum(raised, axis=-1, keepdims=True)
    probs_b = attn_probs.astype(jnp.bfloat16)
    context = jnp.einsum(
        "hqk,khe->qhe", probs_b, value_part, preferred_element_type=jnp.float32
    ).astype(jnp.bfloat16)
    grad_context = context_term.astype(jnp.bfloat16).reshape(seq_len, head_count, head_width)
    grad_prob = jnp.einsum(
        "qhe,khe->hqk", grad_context, value_part, preferred_element_type=jnp.float32
    )
    row_dot = jnp.sum(attn_probs * grad_prob, axis=-1, keepdims=True)
    grad_score = (attn_probs * (grad_prob - row_dot) * score_scale).astype(jnp.bfloat16)
    grad_values = jnp.einsum(
        "hqk,qhe->khe", probs_b, grad_context, preferred_element_type=jnp.float32
    ).astype(jnp.bfloat16)
    grad_queries = jnp.einsum(
        "hqk,khe->qhe", grad_score, key_part, preferred_element_type=jnp.float32
    ).astype(jnp.bfloat16)
    grad_keys = jnp.einsum(
        "hqk,qhe->khe", grad_score, queries, preferred_element_type=jnp.float32
    ).astype(jnp.bfloat16)
    grad_rows = jnp.concatenate([grad_queries, grad_keys, grad_values], axis=-1)
    grad_rows = grad_rows.reshape(seq_len, qkv_width)
    context_flat = context.reshape(seq_len, head_count * head_width)
    summed = lax.psum_scatter(
        jnp.concatenate(
            [
                rows_product(normalized_full_rows, grad_rows),
                rows_product(upstream_grad, context_flat),
            ],
            axis=1,
        ).astype(jnp.bfloat16),
        "dp",
        scatter_dimension=0,
        tiled=True,
    ).astype(jnp.float32)
    grad_qkv = summed[:, :qkv_width]
    grad_out = summed[:, qkv_width:]
    normalized_rows_gradient = lax.psum_scatter(
        jnp.dot(grad_rows, qkv_whole.T, preferred_element_type=jnp.float32).astype(jnp.bfloat16),
        "tensor",
        scatter_dimension=0,
        tiled=True,
    ).astype(jnp.float32)
    first_row_index = lax.axis_index("tensor") * row_block_span
    owned_standardized_input = lax.dynamic_slice_in_dim(
        standardized_input, first_row_index, row_block_span, 0
    )
    owned_inverse_deviation = lax.dynamic_slice_in_dim(
        inverse_deviation, first_row_index, row_block_span, 0
    )
    gradient_average = jnp.mean(normalized_rows_gradient, axis=-1, keepdims=True)
    projection_average = jnp.mean(
        normalized_rows_gradient * owned_standardized_input, axis=-1, keepdims=True
    )
    hidden_input_gradient = (
        owned_inverse_deviation
        * (
            normalized_rows_gradient
            - gradient_average
            - owned_standardized_input * projection_average
        )
    ).astype(jnp.bfloat16)
    grad_qkv = (grad_qkv / n_data).reshape(piece_rows, head_count, 3 * head_width)
    grad_out = (grad_out / n_data).reshape(piece_rows, head_count, head_width)
    return (hidden_input_gradient, grad_qkv, grad_out)


def solution(mesh):
    in_specs = (P("dp", None), P("dp", "tensor", None), P("dp", "tensor", None), P("dp", None))
    out_specs = (P(("dp", "tensor"), None), P("dp", "tensor", None), P("dp", "tensor", None))
    return jax.shard_map(
        per_device, mesh=mesh, in_specs=in_specs, out_specs=out_specs, check_vma=False
    )
```

profile of v0, /device:TPU:1, one launch (start us, length us, event | category | flops | bytes accessed | tf_op | source)
XLA Modules:
  0.0 468.6 jit_solution(1589735804060104992)
XLA Ops:
  7.2 0.0 copy-start
  7.2 0.0 all-gather.5.cloned.1.call-start
  7.2 0.7 all-gather.5.cloned.1.call-update
  7.9 0.0 all-gather.3.cloned.1.call-start
  8.0 2.1 copy.38
  10.1 0.0 all-gather.3.cloned.1.call-update
  10.1 0.0 reduce-scatter.5.cloned.1.call-start
  10.1 2.4 convert_reduce_fusion
  12.5 2.9 fusion.5
  15.4 36.9 %all-gather.5.cloned.1.call-done = bf16[6144,2,128]{2,1,0:T(2,128)(2,1)} async-done(((bf16[384,2,128]{2,1,0:T(2,128)(2,1)}), bf16[6144,2,128]{2,1,0:T(2,128)(2,1)}) %all-gather.5.cloned.1.call-update) | async-done | bytes 3145744 | tf_op jit(solution)/shard_map/all_gather | solution.py:39
  52.3 0.0 copy-done
  52.3 3.9 fusion.20
  56.2 58.5 %all-gather.3.cloned.1.call-done = bf16[6144,2,384]{2,0,1:T(8,128)(2,1)} async-done(((bf16[384,2,384]{2,0,1:T(8,128)(2,1)}), bf16[6144,2,384]{2,0,1:T(8,128)(2,1)}) %all-gather.3.cloned.1.call-update) | async-done | bytes 9437200 | tf_op jit(solution)/shard_map/all_gather | solution.py:38
  114.7 12.7 %copy.39 = bf16[6144,2,384]{0,2,1:T(8,128)(2,1)} copy(bf16[6144,2,384]{2,0,1:T(8,128)(2,1)} %all-gather.3.cloned.1.call-done) | data formatting | bytes 18874368 | tf_op jit(solution)/shard_map/all_gather | solution.py:38
  127.4 8.1 %fusion.12 = bf16[256,768]{1,0:T(8,128)(2,1)} fusion(bf16[6144,768]{0,1:T(8,128)(2,1)} %bitcast.37, bf16[256,6144]{1,0:T(8,128)(2,1)} %param.4, f32[256]{0:T(256)S(1)} %add_rsqrt_fusion, f32[256]{0:T(256)S(1)} %broadcast_multiply_fusion), kind=kOutput, calls=%fused_computation.18 | convolution fusion | flops 2422407168 | bytes 12978176 | tf_op jit(solution)/shard_map/dot_general | solution.py:43
  135.5 1.1 reshape.68
  136.6 0.9 fusion.60
  137.5 0.0 copy-start.3
  137.5 0.0 copy-start.4
  137.5 0.6 copy-done.3
  138.2 0.1 copy-done.4
  138.2 1.0 fusion.15
  139.3 2.0 fusion.35
  141.3 2.0 fusion.41
  143.3 1.9 fusion.24
  145.1 0.0 copy-start.5
  145.1 1.9 fusion.23
  147.0 0.0 copy-start.6
  147.0 1.7 fusion.25
  148.7 0.0 copy-start.7
  148.7 11.4 %fusion.1 = bf16[256,6144]{1,0:T(8,128)(2,1)} fusion(bf16[6144,2,384]{2,0,1:T(8,128)(2,1)} %all-gather.3.cloned.1.call-done, bf16[256,2,128]{0,2,1:T(8,128)(2,1)S(1)} %fusion.25, bf16[256,2,128]{0,2,1:T(8,128)(2,1)S(1)} %fusion.24, bf16[256,2,128]{0,2,1:T(8,128)(2,1)S(1)} %fusion.23), kind=kOutput, calls=%fused_computation.7 | convolution fusion | flops 2418671616 | bytes 12976128 | tf_op jit(solution)/shard_map/dot_general | solution.py:92
  160.1 0.0 copy-done.5
  160.1 0.0 copy-done.6
  160.1 0.0 copy-done.7
  160.1 0.0 reduce-scatter.5.cloned.1.call-update
  160.1 0.2 reduce-scatter.7.cloned.1.call-start
  160.4 1.1 pad_maximum_fusion.1
  161.4 2.3 convolution_convert_fusion.2
  163.7 0.0 copy-start.2
  163.7 2.0 fusion.4
  165.8 0.0 copy-done.2
  165.8 3.2 convolution_convert_fusion
  169.0 5.4 %pad_maximum_fusion = bf16[6144,1024]{0,1:T(8,128)(2,1)} fusion(bf16[6144,256]{0,1:T(8,128)(2,1)S(1)} %fusion.4, bf16[6144,768]{0,1:T(8,128)(2,1)S(1)} %convolution_convert_fusion), kind=kLoop, calls=%fused_computation.1 | loop fusion | flops 25165824 | bytes 25165824 | tf_op jit(solution)/shard_map/concatenate | solution.py:78
  174.4 16.6 %copy.63 = bf16[6144,1024]{1,0:T(8,128)(2,1)} copy(bf16[6144,1024]{0,1:T(8,128)(2,1)} %pad_maximum_fusion) | data formatting | bytes 25165824
  191.1 0.0 reduce-scatter.7.cloned.1.call-update
  191.1 0.1 dynamic-slice.3
  191.2 0.0 copy-start.1
  191.2 5.8 %fusion.2 = f32[256,6144]{1,0:T(8,128)} fusion(bf16[256,6144]{1,0:T(8,128)(2,1)} %param.4, f32[256]{0:T(256)S(1)} %add_rsqrt_fusion, f32[256]{0:T(256)S(1)} %broadcast_multiply_fusion), kind=kLoop, calls=%fused_computation.8 | loop fusion | flops 4718592 | bytes 9439232 | tf_op jit(solution)/shard_map/mul | solution.py:15
  197.0 169.8 %reduce-scatter.5.cloned.1.call-done = bf16[16,6144]{1,0:T(8,128)(2,1)} async-done(((bf16[256,6144]{1,0:T(8,128)(2,1)}), bf16[16,6144]{1,0:T(8,128)(2,1)}) %reduce-scatter.5.cloned.1.call-update) | async-done | bytes 196624 | tf_op jit(solution)/shard_map/reduce_scatter | solution.py:91
  366.8 1.3 convert_reduce_fusion.1
  368.1 1.9 fusion.32
  370.0 83.2 %reduce-scatter.7.cloned.1.call-done = bf16[384,1024]{1,0:T(8,128)(2,1)} async-done(((bf16[6144,1024]{1,0:T(8,128)(2,1)}), bf16[384,1024]{1,0:T(8,128)(2,1)}) %reduce-scatter.7.cloned.1.call-update) | async-done | bytes 786448
  453.1 2.3 copy.64
  455.4 1.2 convert_element_type.72
  456.7 1.1 slice_multiply_fusion
  457.8 3.4 copy.52
  461.2 0.9 copy.53
  462.1 0.0 copy-done.1
  (4 shorter events, 0.0 us)
Async XLA Ops:
  7.2 45.2 %copy-start = (bf16[256,6144]{1,0:T(8,128)(2,1)S(1)}, bf16[256,6144]{1,0:T(8,128)(2,1)}, u32[]{:S(2)}) copy-start(bf16[256,6144]{1,0:T(8,128)(2,1)} %param.7) | copy-start | bytes 9437188
  7.2 45.1 %all-gather.5.cloned.1.call-start = ((), (), s32[]{:S(2)}) async-start(), calls=%async_computation.3 | async-start | bytes 3342336 | tf_op jit(solution)/shard_map/all_gather | solution.py:39
  7.9 106.8 %all-gather.3.cloned.1.call-start = ((), (), s32[]{:S(2)}) async-start(), calls=%async_computation.2 | async-start | bytes 10027008 | tf_op jit(solution)/shard_map/all_gather | solution.py:38
  10.1 356.7 %reduce-scatter.5.cloned.1.call-start = ((), (), s32[]{:S(2)}) async-start(), calls=%async_computation.4 | async-start | bytes 3342336 | tf_op jit(solution)/shard_map/reduce_scatter | solution.py:91
  137.5 0.7 copy-start.3
  137.5 0.7 copy-start.4
  145.1 15.0 %copy-start.5 = (bf16[256,2,128]{0,2,1:T(8,128)(2,1)}, bf16[256,2,128]{0,2,1:T(8,128)(2,1)S(1)}, u32[]{:S(2)}) copy-start(bf16[256,2,128]{0,2,1:T(8,128)(2,1)S(1)} %fusion.24) | copy-start | bytes 393220
  147.0 13.1 %copy-start.6 = (bf16[256,2,128]{0,2,1:T(8,128)(2,1)}, bf16[256,2,128]{0,2,1:T(8,128)(2,1)S(1)}, u32[]{:S(2)}) copy-start(bf16[256,2,128]{0,2,1:T(8,128)(2,1)S(1)} %fusion.23) | copy-start | bytes 393220
  148.7 11.4 %copy-start.7 = (bf16[256,2,128]{0,2,1:T(8,128)(2,1)}, bf16[256,2,128]{0,2,1:T(8,128)(2,1)S(1)}, u32[]{:S(2)}) copy-start(bf16[256,2,128]{0,2,1:T(8,128)(2,1)S(1)} %fusion.25) | copy-start | bytes 393220
  160.1 293.0 %reduce-scatter.7.cloned.1.call-start = ((), (), s32[]{:S(2)}) async-start(), calls=%async_computation.5 | async-start | bytes 13369344
  163.7 2.0 copy-start.2
  191.2 270.9 %copy-start.1 = (bf16[256,6144]{1,0:T(8,128)(2,1)S(1)}, bf16[256,6144]{1,0:T(8,128)(2,1)}, u32[]{:S(2)}) copy-start(bf16[256,6144]{1,0:T(8,128)(2,1)} %param.7) | copy-start | bytes 9437188
Sparse Core Ops, SparseCore 0:
  9.9 42.4 all-gather.4
  54.7 59.9 all-gather.2
  160.3 206.4 reduce-scatter.4
  369.4 83.7 reduce-scatter.6
where the time goes:
time: 472 us; the launch traced here: 469 us
  waiting for transfers between devices  349 us (74%)
  matrix products  41.4 us (9%)
  local copies, waits for them, and re-layouts  40.9 us (9%)
  other arithmetic  23.1 us (5%)
  between operations  13.9 us (3%)
    reduce_scatter x1, waiting for transfers between devices, per_device(): lax.psum_scatter(jnp.dot(grad_rows, qkv_whole.T, preferred_element_type=j...  170 us
    unnamed x5, waiting for transfers between devices  83.9 us
    all_gather x1, waiting for transfers between devices, per_device(): lax.all_gather(w_qkv, 'dp', axis=0, tiled=True)  58.5 us
    all_gather x1, waiting for transfers between devices, per_device(): lax.all_gather(w_out, 'dp', axis=0, tiled=True)  36.9 us
    unnamed x21, local copies, waits for them, and re-layouts  26 us
    all_gather x1, local copies, waits for them, and re-layouts, per_device(): lax.all_gather(w_qkv, 'dp', axis=0, tiled=True)  12.7 us
    dot_general x1, matrix products, per_device(): jnp.dot(grad_rows, qkv_whole.T, preferred_element_type=jnp.float32)  11.4 us
  transfers between devices with their start and end apart: 4, of which 4 were waited for; matrix products, arithmetic and copies ran while one was open for 11% of the time, Pallas kernels for 0%

commit v1 on v0

v1 whole, which is shorter than its diff:
```python
import math

import jax
import jax.numpy as jnp
from jax import lax
from jax.experimental import pallas as pl
from jax.experimental.pallas import tpu as pltpu
from jax.sharding import PartitionSpec as P

EPS = 1e-05
MESH = pl.DeviceIdType.MESH
BF16 = jnp.bfloat16
F32 = jnp.float32

D = 6144
ROWS = 384
SEQ = 256
HEAD = 128
CHIP_D = 2 * ROWS
QW = 3 * HEAD
N_CHIPS = 8
N_DP = 16
GROUPS = 4
N_MESSAGES = 200

GATHER_A, GATHER_A0, GATHER_B0 = 160, 80, 112
SCATTER_A = {QW: 160, HEAD: 48}


def mm(a, b):
    return lax.dot_general(a, b, (((1,), (0,)), ((), ())), preferred_element_type=F32)


def mm_nt(a, b):
    return lax.dot_general(a, b, (((1,), (1,)), ((), ())), preferred_element_type=F32)


def standardize(rows):
    centered = rows - jnp.mean(rows, axis=-1, keepdims=True)
    inverse_deviation = lax.rsqrt(jnp.mean(centered * centered, axis=-1, keepdims=True) + EPS)
    return centered * inverse_deviation, inverse_deviation


def kernel(
    x_hbm, wq_hbm, wo_hbm, up_hbm,
    hid_out, gq_out, go_out,
    wq, wo, nrm, up, xbuf, xrow, acc_q, acc_o, qkv, probs, rows_t, rows, ctx_t,
    gq, go,
    q_ya, q_xa1, q_xa2, q_xb1, q_xb2, q_yb,
    o_ya, o_xa1, o_xa2, o_xb1, o_xb2, o_yb,
    sq_send, sq_recv, so_send, so_recv,
    gn, gns, gnr, zr0, zr1, ysend, yrecv, gnf, xhat, inv,
    local_sem, send_sem, recv_sem,
):
    dp = lax.axis_index("dp")
    tn = lax.axis_index("tensor")
    core = lax.rem(dp, 2)
    other = 1 - core
    x = lax.rem(lax.div(dp, 2), 4)
    y = lax.div(dp, 8)
    z = lax.rem(tn, 8)
    yh = lax.div(tn, 8)

    def dp_at(yy, xx, cc):
        return (yy * 4 + xx) * 2 + cc

    sib = (dp_at(y, x, other), tn)
    xp = (dp_at(y, lax.rem(x + 1, 4), core), tn)
    xm = (dp_at(y, lax.rem(x + 3, 4), core), tn)
    yp = (dp_at(1 - y, x, core), tn)
    zp = (dp, yh * 8 + lax.rem(z + 1, 8))
    zm = (dp, yh * 8 + lax.rem(z + 7, 8))
    yhp = (dp, (1 - yh) * 8 + z)
    partners = (sib, xp, xm, yp, zp, zm, yhp)

    messages = []

    def send(src, dst, target):
        k = len(messages)
        copy = pltpu.make_async_remote_copy(
            src_ref=src, dst_ref=dst, send_sem=send_sem.at[k], recv_sem=recv_sem.at[k],
            device_id=target, device_id_type=MESH,
        )
        copy.start()
        messages.append(copy)
        return copy

    def chip_cols(slot):
        dy, dx = lax.div(slot, 4), lax.rem(slot, 4)
        chip = lax.rem(y + dy, 2) * 4 + lax.rem(x + dx, 4)
        return pl.ds(pl.multiple_of(chip * CHIP_D, 128), CHIP_D)

    def add_rows(n_rows, dst, *srcs):
        def body(r, carry):
            at = pl.ds(pl.multiple_of(r * 16, 16), 16)
            total = dst(at)[...].astype(F32)
            for src in srcs:
                total = total + src(at)[...].astype(F32)
            dst(at)[...] = total.astype(BF16)
            return carry

        lax.fori_loop(0, n_rows // 16, body, 0)

    barrier = pltpu.get_barrier_semaphore()
    for partner in partners:
        pl.semaphore_signal(barrier, inc=1, device_id=partner, device_id_type=MESH)
    token0 = pl.multiple_of(tn * 16, 16)
    loads = [
        pltpu.make_async_copy(x_hbm, xbuf, local_sem.at[0]),
        pltpu.make_async_copy(x_hbm.at[pl.ds(token0, 16)], xrow, local_sem.at[1]),
        pltpu.make_async_copy(wq_hbm.at[core], wq.at[0, core], local_sem.at[2]),
        pltpu.make_async_copy(wo_hbm.at[core], wo.at[0, core], local_sem.at[3]),
        pltpu.make_async_copy(up_hbm, up.at[0], local_sem.at[4]),
    ]
    for load in loads[:4]:
        load.start()
    pl.semaphore_wait(barrier, len(partners))

    A = pl.ds(0, GATHER_A)
    A0 = pl.ds(0, GATHER_A0)
    A1 = pl.ds(GATHER_A0, GATHER_A - GATHER_A0)
    B = pl.ds(GATHER_A, ROWS - GATHER_A)
    B0 = pl.ds(GATHER_A, GATHER_B0)
    B1 = pl.ds(GATHER_A + GATHER_B0, ROWS - GATHER_A - GATHER_B0)

    class Gather:
        def __init__(self, w, w_hbm, load):
            self.w, self.w_hbm, self.load = w, w_hbm, load

        def stage0(self):
            w, src = self.w, self.w_hbm
            self.swap = send(src.at[other], w.at[0, core], sib)
            self.xa_p = [send(src.at[core, A], w.at[3, core, A], xp)]
            self.xa_m = [send(src.at[core, A], w.at[1, core, A], xm)]
            self.yb = [send(src.at[core, B], w.at[4, core, B], yp)]

        def stage0b(self):
            w = self.w
            self.swap.wait_recv()
            self.xa_p.append(send(w.at[0, other, A], w.at[3, other, A], xp))
            self.xa_m.append(send(w.at[0, other, A], w.at[1, other, A], xm))
            self.yb.append(send(w.at[0, other, B], w.at[4, other, B], yp))
            self.load.wait()
            self.xb_p = send(w.at[0, :, B], w.at[3, :, B], xp)
            self.xb_m = send(w.at[0, :, B], w.at[1, :, B], xm)
            self.ya = [send(w.at[0, :, A], w.at[4, :, A], yp)]

        def stage1(self):
            w = self.w
            for m in self.xa_p:
                m.wait_recv()
            self.xa2_p = send(w.at[3, :, A0], w.at[2, :, A0], xp)
            for m in self.xa_m:
                m.wait_recv()
            self.xa2_m = send(w.at[1, :, A1], w.at[2, :, A1], xm)
            self.ya.append(send(w.at[3, :, A], w.at[7, :, A], yp))
            self.ya.append(send(w.at[1, :, A], w.at[5, :, A], yp))

        def stage2(self):
            w = self.w
            for m in self.yb:
                m.wait_recv()
            self.xb3_p = send(w.at[4, :, B], w.at[7, :, B], xp)
            self.xb3_m = send(w.at[4, :, B], w.at[5, :, B], xm)

        def stage3(self):
            w = self.w
            self.xb_p.wait_recv()
            self.xb2_p = send(w.at[3, :, B0], w.at[2, :, B0], xp)
            self.xb_m.wait_recv()
            self.xb2_m = send(w.at[1, :, B1], w.at[2, :, B1], xm)

        def stage4(self):
            w = self.w
            self.xa2_p.wait_recv()
            self.ya.append(send(w.at[2, :, A0], w.at[6, :, A0], yp))
            self.xa2_m.wait_recv()
            self.ya.append(send(w.at[2, :, A1], w.at[6, :, A1], yp))

        def stage5(self):
            w = self.w
            self.xb3_p.wait_recv()
            self.xb4_p = send(w.at[7, :, B0], w.at[6, :, B0], xp)
            self.xb3_m.wait_recv()
            self.xb4_m = send(w.at[5, :, B1], w.at[6, :, B1], xm)

        def finish(self):
            for m in (self.xb2_p, self.xb2_m, *self.ya, self.xb4_p, self.xb4_m):
                m.wait_recv()

    g_q = Gather(wq, wq_hbm, loads[2])
    g_o = Gather(wo, wo_hbm, loads[3])
    g_q.stage0()
    g_q.stage0b()

    loads[4].start()
    up_msg = send(up_hbm, up.at[1], sib)
    loads[0].wait()

    def norm_rows(r, carry):
        at = pl.ds(pl.multiple_of(r * 16, 16), 16)
        standardized, _ = standardize(xbuf[at, :].astype(F32))
        nrm[0, at, :] = standardized.astype(BF16)
        return carry

    lax.fori_loop(0, SEQ // 16, norm_rows, 0)
    nrm_msg = send(nrm.at[0], nrm.at[1], sib)

    g_q.stage1()
    g_q.stage2()

    loads[1].wait()
    own_xhat, own_inv = standardize(xrow[...].astype(F32))
    xhat[...] = own_xhat
    inv[...] = jnp.broadcast_to(own_inv, (16, 128))

    g_q.stage3()
    g_o.stage0()
    g_o.stage0b()
    g_q.stage4()
    g_q.stage5()
    nrm_msg.wait_recv()
    g_q.finish()

    def project(acc, w, left, width):
        acc[...] = jnp.zeros_like(acc)

        def body(slot, carry):
            a = left[:, :, chip_cols(slot)].reshape(2 * SEQ, CHIP_D)
            b = w[slot].reshape(CHIP_D, width)
            acc[...] += mm(a, b)
            return carry

        lax.fori_loop(0, N_CHIPS, body, 0)

    project(acc_q, wq, nrm, QW)
    qkv[...] = acc_q[...].astype(BF16)
    g_o.stage1()
    g_o.stage2()

    scale = 1.0 / math.sqrt(HEAD)

    def forward(s):
        at = pl.ds(s * SEQ, SEQ)
        query, key, value = (qkv[at, pl.ds(n * HEAD, HEAD)] for n in range(3))
        raised = jnp.exp(mm_nt(query, key) * scale)
        attn = raised / jnp.sum(raised, axis=-1, keepdims=True)
        probs[s] = attn
        context = mm(attn.astype(BF16), value).astype(BF16).astype(F32)
        ctx_t[:, at] = context.T.astype(BF16)

    forward(0)
    g_o.stage3()
    g_o.stage4()
    forward(1)
    g_o.stage5()

    loads[4].wait()
    up_msg.wait_recv()

    def weight_unit(g, left_t, right, slot):
        b = right[:, :, chip_cols(slot)].reshape(2 * SEQ, CHIP_D)
        g[slot] = mm(left_t[...], b).astype(BF16)

    L = (pl.ds(0, ROWS), pl.ds(ROWS, ROWS))

    class Scatter:
        def __init__(self, g, width, ya, xa1, xa2, xb1, xb2, yb):
            self.g, self.width = g, width
            self.na = SCATTER_A[width]
            self.nb = width - self.na
            self.A, self.B = pl.ds(0, self.na), pl.ds(self.na, self.nb)
            self.ya, self.xa1, self.xa2, self.xb1, self.xb2, self.yb = ya, xa1, xa2, xb1, xb2, yb
            self.m = {}

        def rows_a(self, slot, lanes=slice(None)):
            return lambda at: self.g.at[slot, at, lanes]

        def rows_b(self, slot, lanes=slice(None)):
            def view(at):
                return self.g.at[slot, pl.ds(pl.multiple_of(at.start + self.na, 16), 16), lanes]

            return view

        def send_ya(self, dx):
            self.m["ya", dx] = send(self.g.at[4 + dx, self.A], self.ya.at[dx], yp)

        def send_xb1(self, dy):
            for n, target in enumerate((xp, xm)):
                self.m["xb1", dy, n] = send(
                    self.g.at[dy * 4 + 2, self.B, L[n]], self.xb1.at[dy, n], target
                )

        def step_xb2(self, dy):
            for n, (slot, target) in enumerate(((1, xp), (3, xm))):
                self.m["xb1", dy, n].wait_recv()
                add_rows(
                    self.nb, self.rows_b(dy * 4 + slot, L[n]),
                    lambda at, n=n: self.xb1.at[dy, n, at],
                )
                self.m["xb2", dy, n] = send(
                    self.g.at[dy * 4 + slot, self.B], self.xb2.at[dy, n], target
                )

        def step_xa1(self):
            self.m["ya", 2].wait_recv()
            add_rows(self.na, self.rows_a(2), lambda at: self.ya.at[2, at])
            for n, target in enumerate((xp, xm)):
                self.m["xa1", n] = send(self.g.at[2, self.A, L[n]], self.xa1.at[n], target)

        def step_xa2(self):
            for n, (slot, target) in enumerate(((1, xp), (3, xm))):
                self.m["ya", slot].wait_recv()
                self.m["xa1", n].wait_recv()
                add_rows(
                    self.na, self.rows_a(slot, L[n]),
                    lambda at, n=n, slot=slot: self.ya.at[slot, at, L[n]],
                    lambda at, n=n: self.xa1.at[n, at],
                )
                add_rows(
                    self.na, self.rows_a(slot, L[1 - n]),
                    lambda at, n=n, slot=slot: self.ya.at[slot, at, L[1 - n]],
                )
                self.m["xa2", n] = send(self.g.at[slot, self.A], self.xa2.at[n], target)

        def step_yb(self):
            for n in range(2):
                self.m["xb2", 1, n].wait_recv()
            add_rows(
                self.nb, self.rows_b(4),
                lambda at: self.xb2.at[1, 0, at], lambda at: self.xb2.at[1, 1, at],
            )
            self.m["yb"] = send(self.g.at[4, self.B], self.yb, yp)

        def finish(self, out, out_stride, send_buf, recv_buf):
            for key in (("xb2", 0, 0), ("xb2", 0, 1), ("ya", 0), ("xa2", 0), ("xa2", 1), "yb"):
                self.m[key].wait_recv()

            def total(lanes):
                a = self.g[0, self.A, lanes].astype(F32) + self.ya[0, :, lanes].astype(F32)
                a = a + self.xa2[0, :, lanes].astype(F32) + self.xa2[1, :, lanes].astype(F32)
                b = self.g[0, self.B, lanes].astype(F32) + self.yb[:, lanes].astype(F32)
                b = b + self.xb2[0, 0, :, lanes].astype(F32) + self.xb2[0, 1, :, lanes].astype(F32)
                return jnp.concatenate([a, b], axis=0) * (1.0 / N_DP)

            def lanes_of(cc):
                return pl.ds(pl.multiple_of(cc * ROWS, 128), ROWS)

            send_buf[...] = total(lanes_of(other)).astype(BF16)
            message = send(send_buf, recv_buf, sib)

            def write(value, head):
                for fb in range(self.width // HEAD):
                    block = value[fb * HEAD:(fb + 1) * HEAD, :].T
                    out[pl.ds(fb * 2 + head, ROWS, stride=out_stride), :] = block

            write(total(lanes_of(core)), core)
            message.wait_recv()
            write(recv_buf[...].astype(F32), other)

    s_o = Scatter(go, HEAD, o_ya, o_xa1, o_xa2, o_xb1, o_xb2, o_yb)
    s_q = Scatter(gq, QW, q_ya, q_xa1, q_xa2, q_xb1, q_xb2, q_yb)

    def go_body(slot, carry):
        weight_unit(go, ctx_t, up, slot)
        return carry

    lax.fori_loop(0, N_CHIPS, go_body, 0)
    for dy in range(2):
        s_o.send_xb1(dy)
    for dx in (2, 1, 3, 0):
        s_o.send_ya(dx)

    g_o.finish()
    project(acc_o, wo, up, HEAD)

    def backward(s):
        at = pl.ds(s * SEQ, SEQ)
        query, key, value = (qkv[at, pl.ds(n * HEAD, HEAD)] for n in range(3))
        grad_context = acc_o[at, :].astype(BF16)
        attn = probs[s]
        grad_prob = mm_nt(grad_context, value)
        row_dot = jnp.sum(attn * grad_prob, axis=-1, keepdims=True)
        grad_score = (attn * (grad_prob - row_dot) * scale).astype(BF16)
        query_t = query.astype(F32).T.astype(BF16)
        key_t = key.astype(F32).T.astype(BF16)
        grad_context_t = grad_context.astype(F32).T.astype(BF16)
        parts = (
            mm_nt(key_t, grad_score),
            mm(query_t, grad_score),
            mm(grad_context_t, attn.astype(BF16)),
        )
        for n, part in enumerate(parts):
            rows_t[pl.ds(n * HEAD, HEAD), at] = part.astype(BF16)
            rows[at, pl.ds(n * HEAD, HEAD)] = part.T.astype(BF16)

    backward(0)
    s_o.step_xb2(0)
    backward(1)

    def gn_group(g):
        for slot in (2 * g, 2 * g + 1):
            part = mm_nt(rows[...], wq[slot].reshape(CHIP_D, QW)).astype(BF16)
            gn[slot] = part[:SEQ].reshape(2, 128, CHIP_D)
            gns[slot] = part[SEQ:].reshape(2, 128, CHIP_D)
        return send(gns.at[pl.ds(2 * g, 2)], gnr.at[pl.ds(2 * g, 2)], sib)

    def z_rows(dz):
        return pl.ds(pl.multiple_of(lax.rem(z + dz + 8, 8) * 16, 16), 16)

    zm_msgs = {}
    directions = ((zp, 1), (zm, -1))

    def gn_step0(g, message):
        message.wait_recv()
        for slot in (2 * g, 2 * g + 1):
            for h in range(2):
                add_rows(
                    128, lambda at, slot=slot, h=h: gn.at[slot, h, at],
                    lambda at, slot=slot, h=h: gnr.at[slot, h, at],
                )
        for n, (target, _) in enumerate(directions):
            zm_msgs[g, 0, n] = send(gn.at[2 * g + n, :, z_rows(4)], zr0.at[n, g], target)

    def gn_step(g, step):
        for n, (target, sign) in enumerate(directions):
            at = z_rows(sign * (4 - step))
            zm_msgs[g, step - 1, n].wait_recv()
            if step == 1:
                mine = gn[2 * g + n, :, at, :].astype(F32)
                gn[2 * g + n, :, at, :] = (mine + zr0[n, g].astype(F32)).astype(BF16)
            else:
                mine = gn[pl.ds(2 * g, 2), :, at, :].astype(F32)
                mine = mine + zr1[n, g, step - 2].astype(F32)
                gn[pl.ds(2 * g, 2), :, at, :] = mine.astype(BF16)
            zm_msgs[g, step, n] = send(
                gn.at[pl.ds(2 * g, 2), :, at], zr1.at[n, g, step - 1], target
            )

    def gn_sum(g, which):
        at = z_rows(0)
        pair = pl.ds(2 * g, 2)
        total = gn[pair, which, at, :].astype(F32)
        return total + zr1[0, g, 2, :, which].astype(F32) + zr1[1, g, 2, :, which].astype(F32)

    def gn_exchange(g):
        for n in range(2):
            zm_msgs[g, 3, n].wait_recv()
        ysend[g] = gn_sum(g, 1 - yh).astype(BF16)
        zm_msgs[g, "y"] = send(ysend.at[g], yrecv.at[g], yhp)

    def gn_finish(g):
        zm_msgs[g, "y"].wait_recv()
        total = gn_sum(g, yh) + yrecv[g].astype(F32)
        for n in range(2):
            gnf[:, chip_cols(jnp.int32(2 * g + n))] = total[n]

    def q_units(*slots):
        for slot in slots:
            weight_unit(gq, rows_t, nrm, jnp.int32(slot))

    m0 = gn_group(0)
    q_units(2, 6)
    s_q.send_xb1(0)
    s_q.send_xb1(1)
    s_q.send_ya(2)
    gn_step0(0, m0)
    m1 = gn_group(1)
    s_o.step_xb2(1)
    q_units(5, 7)
    s_q.send_ya(1)
    s_q.send_ya(3)
    gn_step0(1, m1)
    m2 = gn_group(2)
    s_o.step_xa1()
    q_units(1, 3)
    gn_step0(2, m2)
    m3 = gn_group(3)
    s_o.step_xa2()
    q_units(4, 0)
    s_q.send_ya(0)
    gn_step0(3, m3)
    s_o.step_yb()

    gn_step(0, 1)
    gn_step(1, 1)
    s_q.step_xb2(0)
    s_q.step_xb2(1)
    gn_step(2, 1)
    gn_step(3, 1)
    s_q.step_xa1()
    gn_step(0, 2)
    gn_step(1, 2)
    s_q.step_xa2()
    gn_step(2, 2)
    gn_step(3, 2)
    s_o.finish(go_out, 2, so_send, so_recv)
    gn_step(0, 3)
    gn_step(1, 3)
    s_q.step_yb()
    gn_step(2, 3)
    gn_step(3, 3)
    gn_exchange(0)
    gn_exchange(1)
    s_q.finish(gq_out, 6, sq_send, sq_recv)
    gn_exchange(2)
    gn_exchange(3)
    for g in range(GROUPS):
        gn_finish(g)

    total = gnf[...]
    standardized = xhat[...]
    mean_g = jnp.mean(total, axis=-1, keepdims=True)
    mean_p = jnp.mean(total * standardized, axis=-1, keepdims=True)
    hid_out[...] = (inv[:, :1] * (total - mean_g - standardized * mean_p)).astype(BF16)

    for message in messages:
        message.wait_send()


def scatter_buffers(width):
    a = SCATTER_A[width]
    b = width - a
    return [
        pltpu.VMEM((4, a, CHIP_D), BF16),
        pltpu.VMEM((2, a, ROWS), BF16),
        pltpu.VMEM((2, a, CHIP_D), BF16),
        pltpu.VMEM((2, 2, b, ROWS), BF16),
        pltpu.VMEM((2, 2, b, CHIP_D), BF16),
        pltpu.VMEM((b, CHIP_D), BF16),
    ]


def per_device(sublayer_input, w_qkv, w_out, upstream_grad):
    wq = jnp.transpose(w_qkv, (1, 0, 2))
    wo = jnp.transpose(w_out, (1, 0, 2))
    scratch = [
        pltpu.VMEM((N_CHIPS, 2, ROWS, QW), BF16),
        pltpu.VMEM((N_CHIPS, 2, ROWS, HEAD), BF16),
        pltpu.VMEM((2, SEQ, D), BF16),
        pltpu.VMEM((2, SEQ, D), BF16),
        pltpu.VMEM((SEQ, D), BF16),
        pltpu.VMEM((16, D), BF16),
        pltpu.VMEM((2 * SEQ, QW), F32),
        pltpu.VMEM((2 * SEQ, HEAD), F32),
        pltpu.VMEM((2 * SEQ, QW), BF16),
        pltpu.VMEM((2, SEQ, SEQ), F32),
        pltpu.VMEM((QW, 2 * SEQ), BF16),
        pltpu.VMEM((2 * SEQ, QW), BF16),
        pltpu.VMEM((HEAD, 2 * SEQ), BF16),
        pltpu.VMEM((N_CHIPS, QW, CHIP_D), BF16),
        pltpu.VMEM((N_CHIPS, HEAD, CHIP_D), BF16),
        *scatter_buffers(QW),
        *scatter_buffers(HEAD),
        pltpu.VMEM((QW, ROWS), BF16),
        pltpu.VMEM((QW, ROWS), BF16),
        pltpu.VMEM((HEAD, ROWS), BF16),
        pltpu.VMEM((HEAD, ROWS), BF16),
        pltpu.VMEM((N_CHIPS, 2, 128, CHIP_D), BF16),
        pltpu.VMEM((N_CHIPS, 2, 128, CHIP_D), BF16),
        pltpu.VMEM((N_CHIPS, 2, 128, CHIP_D), BF16),
        pltpu.VMEM((2, GROUPS, 2, 16, CHIP_D), BF16),
        pltpu.VMEM((2, GROUPS, 3, 2, 2, 16, CHIP_D), BF16),
        pltpu.VMEM((GROUPS, 2, 16, CHIP_D), BF16),
        pltpu.VMEM((GROUPS, 2, 16, CHIP_D), BF16),
        pltpu.VMEM((16, D), F32),
        pltpu.VMEM((16, D), F32),
        pltpu.VMEM((16, 128), F32),
        pltpu.SemaphoreType.DMA((5,)),
        pltpu.SemaphoreType.DMA((N_MESSAGES,)),
        pltpu.SemaphoreType.DMA((N_MESSAGES,)),
    ]
    any_spec = pl.BlockSpec(memory_space=pl.ANY)
    vmem_spec = pl.BlockSpec(memory_space=pltpu.VMEM)
    hid, gq, go = pl.pallas_call(
        kernel,
        out_shape=(
            jax.ShapeDtypeStruct((16, D), BF16),
            jax.ShapeDtypeStruct((ROWS * 6, HEAD), F32),
            jax.ShapeDtypeStruct((ROWS * 2, HEAD), F32),
        ),
        in_specs=[any_spec] * 4,
        out_specs=(vmem_spec,) * 3,
        scratch_shapes=scratch,
        compiler_params=pltpu.CompilerParams(
            collective_id=0, has_side_effects=True, vmem_limit_bytes=62 * 2**20
        ),
        cost_estimate=pl.CostEstimate(
            flops=10_000_000_000, bytes_accessed=10_000_000, transcendentals=200_000
        ),
    )(sublayer_input, wq, wo, upstream_grad)
    gq = gq.reshape(ROWS, 3, 2, HEAD).transpose(0, 2, 1, 3).reshape(ROWS, 2, QW)
    go = go.reshape(ROWS, 2, HEAD)
    return hid, gq, go


def solution(mesh):
    in_specs = (P("dp", None), P("dp", "tensor", None), P("dp", "tensor", None), P("dp", None))
    out_specs = (P(("dp", "tensor"), None), P("dp", "tensor", None), P("dp", "tensor", None))
    return jax.shard_map(
        per_device, mesh=mesh, in_specs=in_specs, out_specs=out_specs, check_vma=False
    )
```

time: 472 us -> 132 us (0.28)
  waiting for transfers between devices: 349 us -> 0 us
  Pallas kernels: 0 us -> 122 us
  matrix products: 41.4 us -> 0 us
  local copies, waits for them, and re-layouts: 40.9 us -> 9.26 us
  other arithmetic: 23.1 us -> 0 us
  between operations: 13.9 us -> 0.66 us
    reduce_scatter x1 -> x0, waiting for transfers between devices: 170 us -> none  [per_device(): lax.psum_scatter(jnp.dot(grad_rows, qkv_whole.T, preferred_element_type=j...]
    pallas_call x0 -> x1, Pallas kernels: none -> 122 us  [per_device(): pl.pallas_call(kernel, out_shape=(jax.ShapeDtypeStruct((16, D), BF16), ja...]
    all_gather x2 -> x0, waiting for transfers between devices: 95.4 us -> none  [the longest x1 58.5 us: per_device(): lax.all_gather(w_qkv, 'dp', axis=0, tiled=True)]
    unnamed x5 -> x0, waiting for transfers between devices: 83.9 us -> none
    dot_general x11 -> x0, matrix products: 39.3 us -> none  [the longest x1 11.4 us: per_device(): jnp.dot(grad_rows, qkv_whole.T, preferred_element_type=jnp.float32)]
    unnamed x21 -> x9, local copies, waits for them, and re-layouts: 26 us -> 6.92 us
    all_gather x1 -> x0, local copies, waits for them, and re-layouts: 12.7 us -> none  [per_device(): lax.all_gather(w_qkv, 'dp', axis=0, tiled=True)]
    reduce_sum x3 -> x0, other arithmetic: 6.52 us -> none  [the longest x1 2.86 us: apply_layer_norm(): jnp.mean(centered * centered, axis=-1, keepdims=True) + EPS]
  transfers between devices with their start and end apart: 4 -> 0, of which waited for: 4 -> 0; matrix products, arithmetic and copies ran while one was open for 11% -> 0% of each run, Pallas kernels for 0% -> 0%
where the time goes in v1:
time: 132 us; the launch traced here: 131 us
  Pallas kernels  122 us (92%)
  local copies, waits for them, and re-layouts  9.26 us (7%)
    pallas_call x1, Pallas kernels, per_device(): pl.pallas_call(kernel, out_shape=(jax.ShapeDtypeStruct((16, D), BF16), ja...  122 us
    unnamed x9, local copies, waits for them, and re-layouts  6.92 us

profile of v1, /device:TPU:1, one launch (start us, length us, event | category | flops | bytes accessed | tf_op | source)
XLA Modules:
  0.0 131.4 jit_solution(5900097779805139755)
XLA Ops:
  0.6 1.6 %copy.17 = bf16[384,2,128]{2,0,1:T(8,128)(2,1)} copy(bf16[384,2,128]{2,1,0:T(2,128)(2,1)} %param.6) | data formatting | bytes 393216 | tf_op args[2]
  2.3 2.0 %copy.16 = bf16[384,2,384]{2,0,1:T(8,128)(2,1)} copy(bf16[384,2,384]{2,1,0:T(2,128)(2,1)} %param.5) | data formatting | bytes 1179648 | tf_op args[1]
  4.2 121.5 %shard_map.67 = (bf16[16,6144]{1,0:T(8,128)(2,1)}, f32[2304,128]{1,0:T(8,128)}, f32[768,128]{1,0:T(8,128)}) custom-call(bf16[256,6144]{1,0:T(8,128)(2,1)} %x_hbm.1, bf16[2,384,384]{2,1,0:T(8,128)(2,1)} %bitcast.13, bf16[2,384,128]{2,1,0:T(8,128)(2,1)} %bitcast.15, bf16[256,6144]{1,0:T(8,128)(2,1)} %up_hbm.1), custom_call_target="tpu_custom_call" | custom-call | flops 10000000000 | bytes 10000000 | tf_op jit(solution)/shard_map/pallas_call | solution.py:575
  125.7 2.3 %copy.12 = f32[384,3,2,128]{0,3,1,2:T(8,128)S(1)} copy(f32[384,3,2,128]{3,2,1,0:T(2,128)} %bitcast.12) | data formatting | bytes 2359296 | tf_op jit(solution)/shard_map/reshape | solution.py:592
  128.1 0.0 copy-start.1
  128.1 0.0 copy-start
  128.1 1.9 %copy.13 = f32[384,2,384]{2,1,0:T(2,128)} copy(f32[384,2,384]{0,2,1:T(8,128)S(1)} %bitcast.11) | data formatting | bytes 2359296
  130.0 0.0 copy-done.1
  130.0 0.7 copy.20
  130.7 0.0 copy-done
  130.7 0.7 copy.21
Async XLA Ops:
  128.1 1.9 %copy-start.1 = (bf16[16,6144]{1,0:T(8,128)(2,1)S(1)}, bf16[16,6144]{1,0:T(8,128)(2,1)}, u32[]{:S(2)}) copy-start(bf16[16,6144]{1,0:T(8,128)(2,1)} %get-tuple-element.15) | copy-start | bytes 589828
  128.1 2.6 %copy-start = (f32[768,128]{1,0:T(8,128)S(1)}, f32[768,128]{1,0:T(8,128)}, u32[]{:S(2)}) copy-start(f32[768,128]{1,0:T(8,128)} %get-tuple-element.8) | copy-start | bytes 1179652

commit v2 on v1

--- a/solution.py
+++ b/solution.py
@@ -22,6 +22,7 @@
 N_DP = 16
 GROUPS = 4
 N_MESSAGES = 200
+SLOT_ORDER = (0, 3, 1, 4, 7, 5, 2, 6)
 
 GATHER_A, GATHER_A0, GATHER_B0 = 160, 80, 112
 SCATTER_A = {QW: 160, HEAD: 48}
@@ -42,14 +43,14 @@
 
 
 def kernel(
-    x_hbm, wq_hbm, wo_hbm, up_hbm,
+    x_hbm, wq_raw_hbm, wo_raw_hbm, up_hbm,
     hid_out, gq_out, go_out,
-    wq, wo, nrm, up, xbuf, xrow, acc_q, acc_o, qkv, probs, rows_t, rows, ctx_t,
+    wq_raw, wo_raw, wq_own, wo_own, wq, wo, nrm, up, xbuf, xrow, acc_q, acc_o, qkv, probs, rows_t, rows, rows_other, ctx_t,
     gq, go,
     q_ya, q_xa1, q_xa2, q_xb1, q_xb2, q_yb,
     o_ya, o_xa1, o_xa2, o_xb1, o_xb2, o_yb,
     sq_send, sq_recv, so_send, so_recv,
-    gn, gns, gnr, zr0, zr1, ysend, yrecv, gnf, xhat, inv,
+    gn, zr0, zr1, ysend, yrecv, gnf, xhat, inv,
     local_sem, send_sem, recv_sem,
 ):
     dp = lax.axis_index("dp")
@@ -86,7 +87,7 @@
         return copy
 
     def chip_cols(slot):
-        dy, dx = lax.div(slot, 4), lax.rem(slot, 4)
+        dy, dx = slot // 4, slot % 4
         chip = lax.rem(y + dy, 2) * 4 + lax.rem(x + dx, 4)
         return pl.ds(pl.multiple_of(chip * CHIP_D, 128), CHIP_D)
 
@@ -108,11 +109,23 @@
     loads = [
         pltpu.make_async_copy(x_hbm, xbuf, local_sem.at[0]),
         pltpu.make_async_copy(x_hbm.at[pl.ds(token0, 16)], xrow, local_sem.at[1]),
-        pltpu.make_async_copy(wq_hbm.at[core], wq.at[0, core], local_sem.at[2]),
-        pltpu.make_async_copy(wo_hbm.at[core], wo.at[0, core], local_sem.at[3]),
+        pltpu.make_async_copy(wq_raw_hbm, wq_raw, local_sem.at[2]),
+        pltpu.make_async_copy(wo_raw_hbm, wo_raw, local_sem.at[3]),
         pltpu.make_async_copy(up_hbm, up.at[0], local_sem.at[4]),
     ]
-    for load in loads[:4]:
+    for n in (2, 3, 0, 1):
+        loads[n].start()
+    loads[2].wait()
+    for h in range(2):
+        wq_own[h] = wq_raw[:, h, :]
+    loads[3].wait()
+    for h in range(2):
+        wo_own[h] = wo_raw[:, h, :]
+    own_loads = [
+        pltpu.make_async_copy(wq_own.at[core], wq.at[0, core, :, pl.ds(0, QW)], local_sem.at[2]),
+        pltpu.make_async_copy(wo_own.at[core], wo.at[0, core], local_sem.at[3]),
+    ]
+    for load in own_loads:
         load.start()
     pl.semaphore_wait(barrier, len(partners))
 
@@ -124,77 +137,81 @@
     B1 = pl.ds(GATHER_A + GATHER_B0, ROWS - GATHER_A - GATHER_B0)
 
     class Gather:
-        def __init__(self, w, w_hbm, load):
-            self.w, self.w_hbm, self.load = w, w_hbm, load
+        def __init__(self, w, own, load, width):
+            self.w, self.own, self.load, self.lanes = w, own, load, pl.ds(0, width)
+
+        def at(self, slot, rows, part=slice(None)):
+            return self.w.at[slot, part, rows, self.lanes]
+
+        def move(self, slot, rows, to_slot, target):
+            return send(self.at(slot, rows), self.at(to_slot, rows), target)
 
         def stage0(self):
-            w, src = self.w, self.w_hbm
-            self.swap = send(src.at[other], w.at[0, core], sib)
-            self.xa_p = [send(src.at[core, A], w.at[3, core, A], xp)]
-            self.xa_m = [send(src.at[core, A], w.at[1, core, A], xm)]
-            self.yb = [send(src.at[core, B], w.at[4, core, B], yp)]
+            src = self.own
+            self.swap = send(src.at[other], self.at(0, slice(None), core), sib)
+            self.xa_p = [send(src.at[core, A], self.at(3, A, core), xp)]
+            self.xa_m = [send(src.at[core, A], self.at(1, A, core), xm)]
+            self.yb = [send(src.at[core, B], self.at(4, B, core), yp)]
 
         def stage0b(self):
-            w = self.w
             self.swap.wait_recv()
-            self.xa_p.append(send(w.at[0, other, A], w.at[3, other, A], xp))
-            self.xa_m.append(send(w.at[0, other, A], w.at[1, other, A], xm))
-            self.yb.append(send(w.at[0, other, B], w.at[4, other, B], yp))
+            self.xa_p.append(send(self.at(0, A, other), self.at(3, A, other), xp))
+            self.xa_m.append(send(self.at(0, A, other), self.at(1, A, other), xm))
+            self.yb.append(send(self.at(0, B, other), self.at(4, B, other), yp))
             self.load.wait()
-            self.xb_p = send(w.at[0, :, B], w.at[3, :, B], xp)
-            self.xb_m = send(w.at[0, :, B], w.at[1, :, B], xm)
-            self.ya = [send(w.at[0, :, A], w.at[4, :, A], yp)]
+            self.xb_p = self.move(0, B, 3, xp)
+            self.xb_m = self.move(0, B, 1, xm)
+            self.ya0 = self.move(0, A, 4, yp)
 
         def stage1(self):
-            w = self.w
             for m in self.xa_p:
                 m.wait_recv()
-            self.xa2_p = send(w.at[3, :, A0], w.at[2, :, A0], xp)
+            self.xa2_p = self.move(3, A0, 2, xp)
             for m in self.xa_m:
                 m.wait_recv()
-            self.xa2_m = send(w.at[1, :, A1], w.at[2, :, A1], xm)
-            self.ya.append(send(w.at[3, :, A], w.at[7, :, A], yp))
-            self.ya.append(send(w.at[1, :, A], w.at[5, :, A], yp))
+            self.xa2_m = self.move(1, A1, 2, xm)
+            self.ya3 = self.move(3, A, 7, yp)
+            self.ya1 = self.move(1, A, 5, yp)
 
         def stage2(self):
-            w = self.w
             for m in self.yb:
                 m.wait_recv()
-            self.xb3_p = send(w.at[4, :, B], w.at[7, :, B], xp)
-            self.xb3_m = send(w.at[4, :, B], w.at[5, :, B], xm)
+            self.xb3_p = self.move(4, B, 7, xp)
+            self.xb3_m = self.move(4, B, 5, xm)
 
         def stage3(self):
-            w = self.w
             self.xb_p.wait_recv()
-            self.xb2_p = send(w.at[3, :, B0], w.at[2, :, B0], xp)
+            self.xb2_p = self.move(3, B0, 2, xp)
             self.xb_m.wait_recv()
-            self.xb2_m = send(w.at[1, :, B1], w.at[2, :, B1], xm)
+            self.xb2_m = self.move(1, B1, 2, xm)
 
         def stage4(self):
-            w = self.w
             self.xa2_p.wait_recv()
-            self.ya.append(send(w.at[2, :, A0], w.at[6, :, A0], yp))
+            self.ya2_p = self.move(2, A0, 6, yp)
             self.xa2_m.wait_recv()
-            self.ya.append(send(w.at[2, :, A1], w.at[6, :, A1], yp))
+            self.ya2_m = self.move(2, A1, 6, yp)
 
         def stage5(self):
-            w = self.w
             self.xb3_p.wait_recv()
-            self.xb4_p = send(w.at[7, :, B0], w.at[6, :, B0], xp)
+            self.xb4_p = self.move(7, B0, 6, xp)
             self.xb3_m.wait_recv()
-            self.xb4_m = send(w.at[5, :, B1], w.at[6, :, B1], xm)
-
-        def finish(self):
-            for m in (self.xb2_p, self.xb2_m, *self.ya, self.xb4_p, self.xb4_m):
+            self.xb4_m = self.move(5, B1, 6, xm)
+
+        def complete(self, slot):
+            pending = {
+                0: (), 3: (), 1: (), 4: (self.ya0,),
+                2: (self.xb2_p, self.xb2_m) if slot == 2 else (),
+                7: (self.ya3,), 5: (self.ya1,),
+                6: (self.ya2_p, self.ya2_m, self.xb4_p, self.xb4_m) if slot == 6 else (),
+            }[slot]
+            for m in pending:
                 m.wait_recv()
 
-    g_q = Gather(wq, wq_hbm, loads[2])
-    g_o = Gather(wo, wo_hbm, loads[3])
+    g_q = Gather(wq, wq_own, own_loads[0], QW)
+    g_o = Gather(wo, wo_own, own_loads[1], HEAD)
     g_q.stage0()
     g_q.stage0b()
 
-    loads[4].start()
-    up_msg = send(up_hbm, up.at[1], sib)
     loads[0].wait()
 
     def norm_rows(r, carry):
@@ -206,37 +223,50 @@
     lax.fori_loop(0, SEQ // 16, norm_rows, 0)
     nrm_msg = send(nrm.at[0], nrm.at[1], sib)
 
+    def project(acc, w, left, width, slot):
+        a = left[:, :, chip_cols(slot)].reshape(2 * SEQ, CHIP_D)
+        product = mm(a, w[slot, :, :, pl.ds(0, width)].reshape(CHIP_D, width))
+        if slot == 0:
+            acc[...] = product
+        else:
+            acc[...] += product
+
+    share_msgs = []
+
+    def project_q(slot):
+        g_q.complete(slot)
+        share_msgs.append(send(
+            wq.at[slot, :, :, pl.ds(0, QW)], wq.at[slot, :, :, pl.ds(QW, QW)], sib
+        ))
+        project(acc_q, wq, nrm, QW, slot)
+
+    def project_o(slot):
+        g_o.complete(slot)
+        project(acc_o, wo, up, HEAD, slot)
+
     g_q.stage1()
     g_q.stage2()
-
+    loads[4].start()
+    up_msg = send(up_hbm, up.at[1], sib)
     loads[1].wait()
     own_xhat, own_inv = standardize(xrow[...].astype(F32))
     xhat[...] = own_xhat
     inv[...] = jnp.broadcast_to(own_inv, (16, 128))
-
+    nrm_msg.wait_recv()
+    project_q(0)
     g_q.stage3()
+    project_q(3)
+    g_q.stage4()
+    project_q(1)
+    project_q(4)
+    g_q.stage5()
     g_o.stage0()
+    project_q(7)
     g_o.stage0b()
-    g_q.stage4()
-    g_q.stage5()
-    nrm_msg.wait_recv()
-    g_q.finish()
-
-    def project(acc, w, left, width):
-        acc[...] = jnp.zeros_like(acc)
-
-        def body(slot, carry):
-            a = left[:, :, chip_cols(slot)].reshape(2 * SEQ, CHIP_D)
-            b = w[slot].reshape(CHIP_D, width)
-            acc[...] += mm(a, b)
-            return carry
-
-        lax.fori_loop(0, N_CHIPS, body, 0)
-
-    project(acc_q, wq, nrm, QW)
+    project_q(5)
+    project_q(2)
+    project_q(6)
     qkv[...] = acc_q[...].astype(BF16)
-    g_o.stage1()
-    g_o.stage2()
 
     scale = 1.0 / math.sqrt(HEAD)
 
@@ -249,14 +279,14 @@
         context = mm(attn.astype(BF16), value).astype(BF16).astype(F32)
         ctx_t[:, at] = context.T.astype(BF16)
 
-    forward(0)
-    g_o.stage3()
-    g_o.stage4()
-    forward(1)
-    g_o.stage5()
-
     loads[4].wait()
     up_msg.wait_recv()
+    forward(0)
+    g_o.stage1()
+    forward(1)
+    g_o.stage2()
+    project_o(0)
+
 
     def weight_unit(g, left_t, right, slot):
         b = right[:, :, chip_cols(slot)].reshape(2 * SEQ, CHIP_D)
@@ -332,7 +362,7 @@
             )
             self.m["yb"] = send(self.g.at[4, self.B], self.yb, yp)
 
-        def finish(self, out, out_stride, send_buf, recv_buf):
+        def finish(self, out, send_buf, recv_buf):
             for key in (("xb2", 0, 0), ("xb2", 0, 1), ("ya", 0), ("xa2", 0), ("xa2", 1), "yb"):
                 self.m[key].wait_recv()
 
@@ -350,9 +380,12 @@
             message = send(send_buf, recv_buf, sib)
 
             def write(value, head):
+                for h in range(2):
+                    pl.when(head == h)(lambda h=h: write_at(value, h))
+
+            def write_at(value, head):
                 for fb in range(self.width // HEAD):
-                    block = value[fb * HEAD:(fb + 1) * HEAD, :].T
-                    out[pl.ds(fb * 2 + head, ROWS, stride=out_stride), :] = block
+                    out[:, head, pl.ds(fb * HEAD, HEAD)] = value[fb * HEAD:(fb + 1) * HEAD, :].T
 
             write(total(lanes_of(core)), core)
             message.wait_recv()
@@ -361,18 +394,30 @@
     s_o = Scatter(go, HEAD, o_ya, o_xa1, o_xa2, o_xb1, o_xb2, o_yb)
     s_q = Scatter(gq, QW, q_ya, q_xa1, q_xa2, q_xb1, q_xb2, q_yb)
 
-    def go_body(slot, carry):
-        weight_unit(go, ctx_t, up, slot)
-        return carry
-
-    lax.fori_loop(0, N_CHIPS, go_body, 0)
-    for dy in range(2):
-        s_o.send_xb1(dy)
-    for dx in (2, 1, 3, 0):
-        s_o.send_ya(dx)
-
-    g_o.finish()
-    project(acc_o, wo, up, HEAD)
+    def o_units(*slots):
+        for slot in slots:
+            weight_unit(go, ctx_t, up, slot)
+
+    g_o.stage3()
+    g_o.stage4()
+    o_units(6, 2)
+    project_o(3)
+    s_o.send_xb1(1)
+    s_o.send_xb1(0)
+    s_o.send_ya(2)
+    g_o.stage5()
+    o_units(5, 7)
+    s_o.send_ya(1)
+    s_o.send_ya(3)
+    project_o(1)
+    project_o(4)
+    o_units(4)
+    s_o.send_ya(0)
+    o_units(1, 3, 0)
+    project_o(7)
+    project_o(5)
+    project_o(2)
+    project_o(6)
 
     def backward(s):
         at = pl.ds(s * SEQ, SEQ)
@@ -392,18 +437,24 @@
         )
         for n, part in enumerate(parts):
             rows_t[pl.ds(n * HEAD, HEAD), at] = part.astype(BF16)
-            rows[at, pl.ds(n * HEAD, HEAD)] = part.T.astype(BF16)
-
+            lanes = pl.ds(n * HEAD, HEAD)
+            if s == 0:
+                rows[:, lanes] = part.T.astype(BF16)
+            else:
+                rows_other[:, lanes] = part.T.astype(BF16)
+
+    s_o.step_xb2(1)
+    backward(1)
+    rows_msg = send(rows_other, rows.at[:, pl.ds(QW, QW)], sib)
+    s_o.step_xb2(0)
     backward(0)
-    s_o.step_xb2(0)
-    backward(1)
 
     def gn_group(g):
         for slot in (2 * g, 2 * g + 1):
-            part = mm_nt(rows[...], wq[slot].reshape(CHIP_D, QW)).astype(BF16)
-            gn[slot] = part[:SEQ].reshape(2, 128, CHIP_D)
-            gns[slot] = part[SEQ:].reshape(2, 128, CHIP_D)
-        return send(gns.at[pl.ds(2 * g, 2)], gnr.at[pl.ds(2 * g, 2)], sib)
+            share_msgs[SLOT_ORDER.index(slot)].wait_recv()
+            part = mm_nt(rows[...], wq[slot].reshape(CHIP_D, 2 * QW)).astype(BF16)
+            gn[slot] = part.reshape(2, 128, CHIP_D)
+        gn_step0(g)
 
     def z_rows(dz):
         return pl.ds(pl.multiple_of(lax.rem(z + dz + 8, 8) * 16, 16), 16)
@@ -411,14 +462,7 @@
     zm_msgs = {}
     directions = ((zp, 1), (zm, -1))
 
-    def gn_step0(g, message):
-        message.wait_recv()
-        for slot in (2 * g, 2 * g + 1):
-            for h in range(2):
-                add_rows(
-                    128, lambda at, slot=slot, h=h: gn.at[slot, h, at],
-                    lambda at, slot=slot, h=h: gnr.at[slot, h, at],
-                )
+    def gn_step0(g):
         for n, (target, _) in enumerate(directions):
             zm_msgs[g, 0, n] = send(gn.at[2 * g + n, :, z_rows(4)], zr0.at[n, g], target)
 
@@ -453,60 +497,57 @@
         zm_msgs[g, "y"].wait_recv()
         total = gn_sum(g, yh) + yrecv[g].astype(F32)
         for n in range(2):
-            gnf[:, chip_cols(jnp.int32(2 * g + n))] = total[n]
+            gnf[:, chip_cols(2 * g + n)] = total[n]
 
     def q_units(*slots):
         for slot in slots:
-            weight_unit(gq, rows_t, nrm, jnp.int32(slot))
-
-    m0 = gn_group(0)
-    q_units(2, 6)
-    s_q.send_xb1(0)
+            weight_unit(gq, rows_t, nrm, slot)
+
+    q_units(6)
     s_q.send_xb1(1)
     s_q.send_ya(2)
-    gn_step0(0, m0)
-    m1 = gn_group(1)
-    s_o.step_xb2(1)
+    rows_msg.wait_recv()
+    gn_group(0)
+    q_units(2)
+    s_q.send_xb1(0)
+    gn_group(1)
+    s_o.step_xa1()
+    gn_step(0, 1)
     q_units(5, 7)
     s_q.send_ya(1)
     s_q.send_ya(3)
-    gn_step0(1, m1)
-    m2 = gn_group(2)
-    s_o.step_xa1()
+    gn_group(2)
+    gn_step(1, 1)
+    gn_step(0, 2)
     q_units(1, 3)
-    gn_step0(2, m2)
-    m3 = gn_group(3)
+    s_q.step_xb2(1)
+    s_q.step_xa1()
+    gn_group(3)
+    gn_step(2, 1)
+    gn_step(1, 2)
+    q_units(4)
+    s_q.send_ya(0)
+    s_o.step_yb()
+    gn_step(0, 3)
+    gn_step(3, 1)
     s_o.step_xa2()
-    q_units(4, 0)
-    s_q.send_ya(0)
-    gn_step0(3, m3)
-    s_o.step_yb()
-
-    gn_step(0, 1)
-    gn_step(1, 1)
-    s_q.step_xb2(0)
-    s_q.step_xb2(1)
-    gn_step(2, 1)
-    gn_step(3, 1)
-    s_q.step_xa1()
-    gn_step(0, 2)
-    gn_step(1, 2)
-    s_q.step_xa2()
     gn_step(2, 2)
-    gn_step(3, 2)
-    s_o.finish(go_out, 2, so_send, so_recv)
-    gn_step(0, 3)
+    q_units(0)
     gn_step(1, 3)
     s_q.step_yb()
+    s_q.step_xa2()
+    gn_exchange(0)
+    gn_step(3, 2)
+    s_q.step_xb2(0)
     gn_step(2, 3)
+    gn_exchange(1)
     gn_step(3, 3)
-    gn_exchange(0)
-    gn_exchange(1)
-    s_q.finish(gq_out, 6, sq_send, sq_recv)
+    s_o.finish(go_out, so_send, so_recv)
     gn_exchange(2)
     gn_exchange(3)
     for g in range(GROUPS):
         gn_finish(g)
+    s_q.finish(gq_out, sq_send, sq_recv)
 
     total = gnf[...]
     standardized = xhat[...]
@@ -531,11 +572,40 @@
     ]
 
 
+def hand_over_kernel(*refs):
+    sources, targets, held, sem = refs[:3], refs[3:6], refs[6:9], refs[9]
+    loads, stores = (
+        [pltpu.make_async_copy(a, b, sem.at[k, n]) for n, (a, b) in enumerate(zip(froms, tos))]
+        for k, (froms, tos) in enumerate(((sources, held), (held, targets)))
+    )
+    for load in loads:
+        load.start()
+    for load, store in zip(loads, stores):
+        load.wait()
+        store.start()
+    for store in stores:
+        store.wait()
+
+
+def hand_over(*arrays):
+    any_spec = pl.BlockSpec(memory_space=pl.ANY)
+    return pl.pallas_call(
+        hand_over_kernel,
+        out_shape=tuple(jax.ShapeDtypeStruct(a.shape, a.dtype) for a in arrays),
+        in_specs=[any_spec] * 3,
+        out_specs=(any_spec,) * 3,
+        scratch_shapes=[pltpu.VMEM(a.shape, a.dtype) for a in arrays]
+        + [pltpu.SemaphoreType.DMA((2, 3))],
+    )(*arrays)
+
+
 def per_device(sublayer_input, w_qkv, w_out, upstream_grad):
-    wq = jnp.transpose(w_qkv, (1, 0, 2))
-    wo = jnp.transpose(w_out, (1, 0, 2))
     scratch = [
-        pltpu.VMEM((N_CHIPS, 2, ROWS, QW), BF16),
+        pltpu.VMEM((ROWS, 2, QW), BF16),
+        pltpu.VMEM((ROWS, 2, HEAD), BF16),
+        pltpu.VMEM((2, ROWS, QW), BF16),
+        pltpu.VMEM((2, ROWS, HEAD), BF16),
+        pltpu.VMEM((N_CHIPS, 2, ROWS, 2 * QW), BF16),
         pltpu.VMEM((N_CHIPS, 2, ROWS, HEAD), BF16),
         pltpu.VMEM((2, SEQ, D), BF16),
         pltpu.VMEM((2, SEQ, D), BF16),
@@ -546,7 +616,8 @@
         pltpu.VMEM((2 * SEQ, QW), BF16),
         pltpu.VMEM((2, SEQ, SEQ), F32),
         pltpu.VMEM((QW, 2 * SEQ), BF16),
-        pltpu.VMEM((2 * SEQ, QW), BF16),
+        pltpu.VMEM((SEQ, 2 * QW), BF16),
+        pltpu.VMEM((SEQ, QW), BF16),
         pltpu.VMEM((HEAD, 2 * SEQ), BF16),
         pltpu.VMEM((N_CHIPS, QW, CHIP_D), BF16),
         pltpu.VMEM((N_CHIPS, HEAD, CHIP_D), BF16),
@@ -556,8 +627,6 @@
         pltpu.VMEM((QW, ROWS), BF16),
         pltpu.VMEM((HEAD, ROWS), BF16),
         pltpu.VMEM((HEAD, ROWS), BF16),
-        pltpu.VMEM((N_CHIPS, 2, 128, CHIP_D), BF16),
-        pltpu.VMEM((N_CHIPS, 2, 128, CHIP_D), BF16),
         pltpu.VMEM((N_CHIPS, 2, 128, CHIP_D), BF16),
         pltpu.VMEM((2, GROUPS, 2, 16, CHIP_D), BF16),
         pltpu.VMEM((2, GROUPS, 3, 2, 2, 16, CHIP_D), BF16),
@@ -576,8 +645,8 @@
         kernel,
         out_shape=(
             jax.ShapeDtypeStruct((16, D), BF16),
-            jax.ShapeDtypeStruct((ROWS * 6, HEAD), F32),
-            jax.ShapeDtypeStruct((ROWS * 2, HEAD), F32),
+            jax.ShapeDtypeStruct((ROWS, 2, QW), F32),
+            jax.ShapeDtypeStruct((ROWS, 2, HEAD), F32),
         ),
         in_specs=[any_spec] * 4,
         out_specs=(vmem_spec,) * 3,
@@ -588,10 +657,8 @@
         cost_estimate=pl.CostEstimate(
             flops=10_000_000_000, bytes_accessed=10_000_000, transcendentals=200_000
         ),
-    )(sublayer_input, wq, wo, upstream_grad)
-    gq = gq.reshape(ROWS, 3, 2, HEAD).transpose(0, 2, 1, 3).reshape(ROWS, 2, QW)
-    go = go.reshape(ROWS, 2, HEAD)
-    return hid, gq, go
+    )(sublayer_input, w_qkv, w_out, upstream_grad)
+    return hand_over(hid, gq, go)
 
 
 def solution(mesh):

time: 132 us -> 108 us (0.82)
  Pallas kernels: 122 us -> 107 us
  local copies, waits for them, and re-layouts: 9.26 us -> 0 us
    pallas_call x1, Pallas kernels: 122 us -> 104 us  [per_device(): pl.pallas_call(kernel, out_shape=(jax.ShapeDtypeStruct((16, D), BF16), ja...]
    unnamed x9 -> x0, local copies, waits for them, and re-layouts: 6.92 us -> none
    pallas_call x0 -> x1, Pallas kernels: none -> 2.57 us  [hand_over(): pl.pallas_call(hand_over_kernel, out_shape=tuple((jax.ShapeDtypeStruct(a....]
    reshape x1 -> x0, local copies, waits for them, and re-layouts: 2.35 us -> none  [per_device(): gq = gq.reshape(ROWS, 3, 2, HEAD).transpose(0, 2, 1, 3).reshape(ROWS, 2, QW)]
where the time goes in v2:
time: 108 us
  Pallas kernels  107 us (99%)
    pallas_call x1, Pallas kernels, per_device(): pl.pallas_call(kernel, out_shape=(jax.ShapeDtypeStruct((16, D), BF16), ja...  104 us
    pallas_call x1, Pallas kernels, hand_over(): pl.pallas_call(hand_over_kernel, out_shape=tuple((jax.ShapeDtypeStruct(a....  2.57 us

profile of v2, /device:TPU:1, one launch (start us, length us, event | category | flops | bytes accessed | tf_op | source)
XLA Modules:
  0.0 107.8 jit_solution(7075718011123301202)
XLA Ops:
  0.6 104.5 %shard_map.67 = (bf16[16,6144]{1,0:T(8,128)(2,1)}, f32[384,2,384]{2,1,0:T(2,128)}, f32[384,2,128]{2,1,0:T(2,128)}) custom-call(bf16[256,6144]{1,0:T(8,128)(2,1)} %x_hbm.1, bf16[384,2,384]{2,1,0:T(2,128)(2,1)} %wq_raw_hbm.1, bf16[384,2,128]{2,1,0:T(2,128)(2,1)} %wo_raw_hbm.1, bf16[256,6144]{1,0:T(8,128)(2,1)} %up_hbm.1), custom_call_target="tpu_custom_call" | custom-call | flops 10000000000 | bytes 10000000 | tf_op jit(solution)/shard_map/pallas_call | solution.py:644
  105.1 2.6 %shard_map.68 = (bf16[16,6144]{1,0:T(8,128)(2,1)}, f32[384,2,384]{2,1,0:T(2,128)}, f32[384,2,128]{2,1,0:T(2,128)}) custom-call(bf16[16,6144]{1,0:T(8,128)(2,1)} %get-tuple-element.6.refs_0_, f32[384,2,384]{2,1,0:T(2,128)} %get-tuple-element.7.refs_1_, f32[384,2,128]{2,1,0:T(2,128)} %get-tuple-element.8.refs_2_), custom_call_target="tpu_custom_call" | custom-call | tf_op jit(solution)/shard_map/pallas_call | solution.py:592

commit v3 on v2

--- a/solution.py
+++ b/solution.py
@@ -47,9 +47,8 @@
     hid_out, gq_out, go_out,
     wq_raw, wo_raw, wq_own, wo_own, wq, wo, nrm, up, xbuf, xrow, acc_q, acc_o, qkv, probs, rows_t, rows, rows_other, ctx_t,
     gq, go,
-    q_ya, q_xa1, q_xa2, q_xb1, q_xb2, q_yb,
-    o_ya, o_xa1, o_xa2, o_xb1, o_xb2, o_yb,
-    sq_send, sq_recv, so_send, so_recv,
+    q_ya, q_xa1, q_xb1, q_xb2, q_own, q_last_ya, q_last_xa, q_last_yb, q_last_xb, q_sum_a,
+    o_ya, o_xa1, o_xb1, o_xb2, o_own, o_last_ya, o_last_xa, o_last_yb, o_last_xb, o_sum_a,
     gn, zr0, zr1, ysend, yrecv, gnf, xhat, inv,
     local_sem, send_sem, recv_sem,
 ):
@@ -72,7 +71,10 @@
     zp = (dp, yh * 8 + lax.rem(z + 1, 8))
     zm = (dp, yh * 8 + lax.rem(z + 7, 8))
     yhp = (dp, (1 - yh) * 8 + z)
-    partners = (sib, xp, xm, yp, zp, zm, yhp)
+    xp_other = (dp_at(y, lax.rem(x + 1, 4), other), tn)
+    xm_other = (dp_at(y, lax.rem(x + 3, 4), other), tn)
+    yp_other = (dp_at(1 - y, x, other), tn)
+    partners = (sib, xp, xm, yp, zp, zm, yhp, xp_other, xm_other, yp_other)
 
     messages = []
 
@@ -279,28 +281,26 @@
         context = mm(attn.astype(BF16), value).astype(BF16).astype(F32)
         ctx_t[:, at] = context.T.astype(BF16)
 
-    loads[4].wait()
-    up_msg.wait_recv()
-    forward(0)
-    g_o.stage1()
-    forward(1)
-    g_o.stage2()
-    project_o(0)
-
-
     def weight_unit(g, left_t, right, slot):
         b = right[:, :, chip_cols(slot)].reshape(2 * SEQ, CHIP_D)
         g[slot] = mm(left_t[...], b).astype(BF16)
 
     L = (pl.ds(0, ROWS), pl.ds(ROWS, ROWS))
 
+    def lanes_of(cc):
+        return pl.ds(pl.multiple_of(cc * ROWS, 128), ROWS)
+
     class Scatter:
-        def __init__(self, g, width, ya, xa1, xa2, xb1, xb2, yb):
+        def __init__(
+            self, g, width, ya, xa1, xb1, xb2, own, last_ya, last_xa, last_yb, last_xb, sum_a
+        ):
             self.g, self.width = g, width
             self.na = SCATTER_A[width]
             self.nb = width - self.na
             self.A, self.B = pl.ds(0, self.na), pl.ds(self.na, self.nb)
-            self.ya, self.xa1, self.xa2, self.xb1, self.xb2, self.yb = ya, xa1, xa2, xb1, xb2, yb
+            self.ya, self.xa1, self.xb1, self.xb2, self.own = ya, xa1, xb1, xb2, own
+            self.last_ya, self.last_xa, self.last_yb, self.last_xb = last_ya, last_xa, last_yb, last_xb
+            self.sum_a = sum_a
             self.m = {}
 
         def rows_a(self, slot, lanes=slice(None)):
@@ -312,8 +312,20 @@
 
             return view
 
+        def last_hop(self, slot, rows, buf, target, target_other):
+            return [
+                send(self.g.at[slot, rows, lanes_of(cc)], buf.at[core], to)
+                for cc, to in ((core, target), (other, target_other))
+            ]
+
+        def send_own(self):
+            self.m["own"] = [send(self.g.at[0, :, lanes_of(other)], self.own, sib)]
+
         def send_ya(self, dx):
-            self.m["ya", dx] = send(self.g.at[4 + dx, self.A], self.ya.at[dx], yp)
+            if dx == 0:
+                self.m["ya", 0] = self.last_hop(4, self.A, self.last_ya, yp, yp_other)
+            else:
+                self.m["ya", dx] = send(self.g.at[4 + dx, self.A], self.ya.at[dx - 1], yp)
 
         def send_xb1(self, dy):
             for n, target in enumerate((xp, xm)):
@@ -322,102 +334,99 @@
                 )
 
         def step_xb2(self, dy):
-            for n, (slot, target) in enumerate(((1, xp), (3, xm))):
+            for n, (slot, target, target_other) in enumerate(((1, xp, xp_other), (3, xm, xm_other))):
                 self.m["xb1", dy, n].wait_recv()
+                at_slot = dy * 4 + slot
                 add_rows(
-                    self.nb, self.rows_b(dy * 4 + slot, L[n]),
-                    lambda at, n=n: self.xb1.at[dy, n, at],
+                    self.nb, self.rows_b(at_slot, L[n]), lambda at, n=n: self.xb1.at[dy, n, at]
                 )
-                self.m["xb2", dy, n] = send(
-                    self.g.at[dy * 4 + slot, self.B], self.xb2.at[dy, n], target
-                )
+                if dy == 0:
+                    self.m["xb2", 0, n] = self.last_hop(
+                        at_slot, self.B, self.last_xb.at[n], target, target_other
+                    )
+                else:
+                    self.m["xb2", 1, n] = send(self.g.at[at_slot, self.B], self.xb2.at[n], target)
 
         def step_xa1(self):
             self.m["ya", 2].wait_recv()
-            add_rows(self.na, self.rows_a(2), lambda at: self.ya.at[2, at])
+            add_rows(self.na, self.rows_a(2), lambda at: self.ya.at[1, at])
             for n, target in enumerate((xp, xm)):
                 self.m["xa1", n] = send(self.g.at[2, self.A, L[n]], self.xa1.at[n], target)
 
         def step_xa2(self):
-            for n, (slot, target) in enumerate(((1, xp), (3, xm))):
+            for n, (slot, target, target_other) in enumerate(((1, xp, xp_other), (3, xm, xm_other))):
                 self.m["ya", slot].wait_recv()
                 self.m["xa1", n].wait_recv()
                 add_rows(
                     self.na, self.rows_a(slot, L[n]),
-                    lambda at, n=n, slot=slot: self.ya.at[slot, at, L[n]],
+                    lambda at, n=n, slot=slot: self.ya.at[slot - 1, at, L[n]],
                     lambda at, n=n: self.xa1.at[n, at],
                 )
                 add_rows(
                     self.na, self.rows_a(slot, L[1 - n]),
-                    lambda at, n=n, slot=slot: self.ya.at[slot, at, L[1 - n]],
+                    lambda at, n=n, slot=slot: self.ya.at[slot - 1, at, L[1 - n]],
                 )
-                self.m["xa2", n] = send(self.g.at[slot, self.A], self.xa2.at[n], target)
+                self.m["xa2", n] = self.last_hop(
+                    slot, self.A, self.last_xa.at[n], target, target_other
+                )
 
         def step_yb(self):
             for n in range(2):
                 self.m["xb2", 1, n].wait_recv()
             add_rows(
                 self.nb, self.rows_b(4),
-                lambda at: self.xb2.at[1, 0, at], lambda at: self.xb2.at[1, 1, at],
+                lambda at: self.xb2.at[0, at], lambda at: self.xb2.at[1, at],
             )
-            self.m["yb"] = send(self.g.at[4, self.B], self.yb, yp)
-
-        def finish(self, out, send_buf, recv_buf):
-            for key in (("xb2", 0, 0), ("xb2", 0, 1), ("ya", 0), ("xa2", 0), ("xa2", 1), "yb"):
-                self.m[key].wait_recv()
-
-            def total(lanes):
-                a = self.g[0, self.A, lanes].astype(F32) + self.ya[0, :, lanes].astype(F32)
-                a = a + self.xa2[0, :, lanes].astype(F32) + self.xa2[1, :, lanes].astype(F32)
-                b = self.g[0, self.B, lanes].astype(F32) + self.yb[:, lanes].astype(F32)
-                b = b + self.xb2[0, 0, :, lanes].astype(F32) + self.xb2[0, 1, :, lanes].astype(F32)
-                return jnp.concatenate([a, b], axis=0) * (1.0 / N_DP)
-
-            def lanes_of(cc):
-                return pl.ds(pl.multiple_of(cc * ROWS, 128), ROWS)
-
-            send_buf[...] = total(lanes_of(other)).astype(BF16)
-            message = send(send_buf, recv_buf, sib)
-
-            def write(value, head):
-                for h in range(2):
-                    pl.when(head == h)(lambda h=h: write_at(value, h))
-
-            def write_at(value, head):
-                for fb in range(self.width // HEAD):
-                    out[:, head, pl.ds(fb * HEAD, HEAD)] = value[fb * HEAD:(fb + 1) * HEAD, :].T
-
-            write(total(lanes_of(core)), core)
-            message.wait_recv()
-            write(recv_buf[...].astype(F32), other)
-
-    s_o = Scatter(go, HEAD, o_ya, o_xa1, o_xa2, o_xb1, o_xb2, o_yb)
-    s_q = Scatter(gq, QW, q_ya, q_xa1, q_xa2, q_xb1, q_xb2, q_yb)
-
-    def o_units(*slots):
-        for slot in slots:
-            weight_unit(go, ctx_t, up, slot)
-
-    g_o.stage3()
-    g_o.stage4()
-    o_units(6, 2)
-    project_o(3)
-    s_o.send_xb1(1)
-    s_o.send_xb1(0)
-    s_o.send_ya(2)
-    g_o.stage5()
-    o_units(5, 7)
-    s_o.send_ya(1)
-    s_o.send_ya(3)
-    project_o(1)
-    project_o(4)
-    o_units(4)
-    s_o.send_ya(0)
-    o_units(1, 3, 0)
-    project_o(7)
-    project_o(5)
-    project_o(2)
-    project_o(6)
+            self.m["yb"] = self.last_hop(4, self.B, self.last_yb, yp, yp_other)
+
+        def total(self, rows, h, *received):
+            mine = self.g[0, rows, lanes_of(core)].astype(F32)
+            total = jnp.where(core == h, mine, self.own[rows, :].astype(F32))
+            for part in received:
+                total = total + part.astype(F32)
+            return total * (1.0 / N_DP)
+
+        def wait_last(self, *keys):
+            for key in keys:
+                for message in self.m[key]:
+                    message.wait_recv()
+
+        def write(self, out, value, fb, h):
+            out[:, h, pl.ds(fb * HEAD, HEAD)] = value.T
+
+        def finish_a(self, out):
+            self.wait_last("own", ("ya", 0), ("xa2", 0), ("xa2", 1))
+            for h in range(2):
+                total = self.total(
+                    self.A, h, self.last_ya[h], self.last_xa[0, h], self.last_xa[1, h]
+                )
+                self.sum_a[h] = total
+                if self.na >= HEAD:
+                    self.write(out, total[:HEAD], 0, h)
+
+        def finish_b(self, out):
+            self.wait_last(("xb2", 0, 0), ("xb2", 0, 1), "yb")
+            done = self.na // HEAD
+            for h in range(2):
+                total = self.total(
+                    self.B, h, self.last_yb[h], self.last_xb[0, h], self.last_xb[1, h]
+                )
+                rest = jnp.concatenate([self.sum_a[h, done * HEAD:, :], total], axis=0)
+                for fb in range(done, self.width // HEAD):
+                    at = (fb - done) * HEAD
+                    self.write(out, rest[at:at + HEAD], fb, h)
+
+    s_o = Scatter(
+        go, HEAD, o_ya, o_xa1, o_xb1, o_xb2, o_own,
+        o_last_ya, o_last_xa, o_last_yb, o_last_xb, o_sum_a,
+    )
+    s_q = Scatter(
+        gq, QW, q_ya, q_xa1, q_xb1, q_xb2, q_own,
+        q_last_ya, q_last_xa, q_last_yb, q_last_xb, q_sum_a,
+    )
+
+    def o_units(slot):
+        weight_unit(go, ctx_t, up, slot)
 
     def backward(s):
         at = pl.ds(s * SEQ, SEQ)
@@ -443,12 +452,6 @@
             else:
                 rows_other[:, lanes] = part.T.astype(BF16)
 
-    s_o.step_xb2(1)
-    backward(1)
-    rows_msg = send(rows_other, rows.at[:, pl.ds(QW, QW)], sib)
-    s_o.step_xb2(0)
-    backward(0)
-
     def gn_group(g):
         for slot in (2 * g, 2 * g + 1):
             share_msgs[SLOT_ORDER.index(slot)].wait_recv()
@@ -499,104 +502,165 @@
         for n in range(2):
             gnf[:, chip_cols(2 * g + n)] = total[n]
 
-    def q_units(*slots):
-        for slot in slots:
-            weight_unit(gq, rows_t, nrm, slot)
-
+    def q_units(slot):
+        weight_unit(gq, rows_t, nrm, slot)
+
+    def norm_backward():
+        total = gnf[...]
+        standardized = xhat[...]
+        mean_g = jnp.mean(total, axis=-1, keepdims=True)
+        mean_p = jnp.mean(total * standardized, axis=-1, keepdims=True)
+        hid_out[...] = (inv[:, :1] * (total - mean_g - standardized * mean_p)).astype(BF16)
+
+    def await_up():
+        loads[4].wait()
+        up_msg.wait_recv()
+
+    settled = []
+
+    def settle(keep):
+        for message in messages[len(settled):len(messages) - keep]:
+            message.wait_send()
+            settled.append(message)
+
+    rows_msgs = []
+
+    def share_rows():
+        rows_msgs.append(send(rows_other, rows.at[:, pl.ds(QW, QW)], sib))
+
+    def await_rows():
+        rows_msgs[0].wait_recv()
+
+    g_o.stage1()
+    g_o.stage2()
+    await_up()
+    project_o(0)
+    forward(0)
+    forward(1)
+    g_o.stage3()
+    o_units(6)
+    o_units(2)
+    s_o.send_ya(2)
+    project_o(4)
+    s_o.send_xb1(1)
+    project_o(3)
+    g_o.stage4()
+    o_units(0)
+    o_units(4)
+    project_o(1)
+    g_o.stage5()
+    project_o(7)
+    s_o.send_xb1(0)
+    s_o.send_ya(0)
+    o_units(1)
+    o_units(7)
+    project_o(5)
+    project_o(2)
+    o_units(5)
+    s_o.send_ya(1)
+    s_o.step_xb2(1)
+    s_o.step_xa1()
+    s_o.send_ya(3)
+    project_o(6)
+    backward(1)
+    share_rows()
+    backward(0)
     q_units(6)
+    s_q.send_ya(2)
     s_q.send_xb1(1)
-    s_q.send_ya(2)
-    rows_msg.wait_recv()
+    await_rows()
+    gn_group(1)
+    q_units(5)
+    gn_group(2)
+    q_units(2)
+    q_units(7)
+    s_q.send_xb1(0)
+    gn_step(1, 1)
+    s_q.send_ya(1)
     gn_group(0)
-    q_units(2)
-    s_q.send_xb1(0)
-    gn_group(1)
-    s_o.step_xa1()
+    gn_step(2, 1)
+    s_q.step_xa1()
+    s_q.send_ya(3)
+    s_q.step_xb2(1)
+    gn_step(1, 2)
+    s_o.send_own()
+    o_units(3)
+    gn_group(3)
     gn_step(0, 1)
-    q_units(5, 7)
-    s_q.send_ya(1)
-    s_q.send_ya(3)
-    gn_group(2)
-    gn_step(1, 1)
+    gn_step(2, 2)
+    q_units(4)
+    q_units(0)
+    s_o.step_xa2()
+    q_units(1)
+    s_q.send_own()
+    s_q.send_ya(0)
+    gn_step(3, 1)
+    q_units(3)
+    gn_step(1, 3)
     gn_step(0, 2)
-    q_units(1, 3)
-    s_q.step_xb2(1)
-    s_q.step_xa1()
-    gn_group(3)
-    gn_step(2, 1)
-    gn_step(1, 2)
-    q_units(4)
-    s_q.send_ya(0)
+    s_o.step_xb2(0)
     s_o.step_yb()
+    s_q.step_xa2()
+    gn_step(3, 2)
+    s_q.step_yb()
+    gn_step(2, 3)
+    s_q.step_xb2(0)
     gn_step(0, 3)
-    gn_step(3, 1)
-    s_o.step_xa2()
-    gn_step(2, 2)
-    q_units(0)
-    gn_step(1, 3)
-    s_q.step_yb()
-    s_q.step_xa2()
+    gn_step(3, 3)
+    s_o.finish_a(go_out)
+    gn_exchange(2)
+    gn_exchange(1)
     gn_exchange(0)
-    gn_step(3, 2)
-    s_q.step_xb2(0)
-    gn_step(2, 3)
-    gn_exchange(1)
-    gn_step(3, 3)
-    s_o.finish(go_out, so_send, so_recv)
-    gn_exchange(2)
+    s_q.finish_a(gq_out)
     gn_exchange(3)
-    for g in range(GROUPS):
-        gn_finish(g)
-    s_q.finish(gq_out, sq_send, sq_recv)
-
-    total = gnf[...]
-    standardized = xhat[...]
-    mean_g = jnp.mean(total, axis=-1, keepdims=True)
-    mean_p = jnp.mean(total * standardized, axis=-1, keepdims=True)
-    hid_out[...] = (inv[:, :1] * (total - mean_g - standardized * mean_p)).astype(BF16)
-
-    for message in messages:
-        message.wait_send()
+    s_o.finish_b(go_out)
+    settle(16)
+    gn_finish(2)
+    gn_finish(1)
+    s_q.finish_b(gq_out)
+    gn_finish(0)
+    gn_finish(3)
+    norm_backward()
+
+    settle(0)
 
 
 def scatter_buffers(width):
     a = SCATTER_A[width]
     b = width - a
     return [
-        pltpu.VMEM((4, a, CHIP_D), BF16),
+        pltpu.VMEM((3, a, CHIP_D), BF16),
         pltpu.VMEM((2, a, ROWS), BF16),
-        pltpu.VMEM((2, a, CHIP_D), BF16),
         pltpu.VMEM((2, 2, b, ROWS), BF16),
-        pltpu.VMEM((2, 2, b, CHIP_D), BF16),
-        pltpu.VMEM((b, CHIP_D), BF16),
+        pltpu.VMEM((2, b, CHIP_D), BF16),
+        pltpu.VMEM((width, ROWS), BF16),
+        pltpu.VMEM((2, a, ROWS), BF16),
+        pltpu.VMEM((2, 2, a, ROWS), BF16),
+        pltpu.VMEM((2, b, ROWS), BF16),
+        pltpu.VMEM((2, 2, b, ROWS), BF16),
+        pltpu.VMEM((2, a, ROWS), F32),
     ]
 
 
 def hand_over_kernel(*refs):
-    sources, targets, held, sem = refs[:3], refs[3:6], refs[6:9], refs[9]
-    loads, stores = (
-        [pltpu.make_async_copy(a, b, sem.at[k, n]) for n, (a, b) in enumerate(zip(froms, tos))]
-        for k, (froms, tos) in enumerate(((sources, held), (held, targets)))
-    )
-    for load in loads:
-        load.start()
-    for load, store in zip(loads, stores):
-        load.wait()
-        store.start()
-    for store in stores:
-        store.wait()
+    sources, targets, sem = refs[:3], refs[3:6], refs[6]
+    copies = [
+        pltpu.make_async_copy(a, b, sem.at[n]) for n, (a, b) in enumerate(zip(sources, targets))
+    ]
+    for copy in copies:
+        copy.start()
+    for copy in copies:
+        copy.wait()
 
 
 def hand_over(*arrays):
-    any_spec = pl.BlockSpec(memory_space=pl.ANY)
     return pl.pallas_call(
         hand_over_kernel,
         out_shape=tuple(jax.ShapeDtypeStruct(a.shape, a.dtype) for a in arrays),
-        in_specs=[any_spec] * 3,
-        out_specs=(any_spec,) * 3,
-        scratch_shapes=[pltpu.VMEM(a.shape, a.dtype) for a in arrays]
-        + [pltpu.SemaphoreType.DMA((2, 3))],
-    )(*arrays)
+        in_specs=[pl.BlockSpec(memory_space=pltpu.VMEM)] * 3,
+        out_specs=(pl.BlockSpec(memory_space=pl.ANY),) * 3,
+        scratch_shapes=[pltpu.SemaphoreType.DMA((3,))],
+    )(*(pltpu.with_memory_space_constraint(a, pltpu.VMEM) for a in arrays))
 
 
 def per_device(sublayer_input, w_qkv, w_out, upstream_grad):
@@ -623,10 +687,6 @@
         pltpu.VMEM((N_CHIPS, HEAD, CHIP_D), BF16),
         *scatter_buffers(QW),
         *scatter_buffers(HEAD),
-        pltpu.VMEM((QW, ROWS), BF16),
-        pltpu.VMEM((QW, ROWS), BF16),
-        pltpu.VMEM((HEAD, ROWS), BF16),
-        pltpu.VMEM((HEAD, ROWS), BF16),
         pltpu.VMEM((N_CHIPS, 2, 128, CHIP_D), BF16),
         pltpu.VMEM((2, GROUPS, 2, 16, CHIP_D), BF16),
         pltpu.VMEM((2, GROUPS, 3, 2, 2, 16, CHIP_D), BF16),
@@ -644,15 +704,15 @@
     hid, gq, go = pl.pallas_call(
         kernel,
         out_shape=(
-            jax.ShapeDtypeStruct((16, D), BF16),
-            jax.ShapeDtypeStruct((ROWS, 2, QW), F32),
-            jax.ShapeDtypeStruct((ROWS, 2, HEAD), F32),
+            pltpu.VMEM((16, D), BF16),
+            pltpu.VMEM((ROWS, 2, QW), F32),
+            pltpu.VMEM((ROWS, 2, HEAD), F32),
         ),
         in_specs=[any_spec] * 4,
         out_specs=(vmem_spec,) * 3,
         scratch_shapes=scratch,
         compiler_params=pltpu.CompilerParams(
-            collective_id=0, has_side_effects=True, vmem_limit_bytes=62 * 2**20
+            collective_id=0, has_side_effects=True, vmem_limit_bytes=61 * 2**20
         ),
         cost_estimate=pl.CostEstimate(
             flops=10_000_000_000, bytes_accessed=10_000_000, transcendentals=200_000

time: 108 us -> 101 us (0.935)
  Pallas kernels: 107 us -> 100 us
    pallas_call x1, Pallas kernels: 104 us -> 99 us  [per_device(): pl.pallas_call(kernel, out_shape=(pltpu.VMEM((16, D), BF16), pltpu.VMEM((...]
    pallas_call x1, Pallas kernels: 2.57 us -> 1.23 us  [hand_over(): pl.pallas_call(hand_over_kernel, out_shape=tuple((jax.ShapeDtypeStruct(a....]
where the time goes in v3:
time: 101 us
  Pallas kernels  100 us (99%)
    pallas_call x1, Pallas kernels, per_device(): pl.pallas_call(kernel, out_shape=(pltpu.VMEM((16, D), BF16), pltpu.VMEM((...  99 us

profile of v3, /device:TPU:1, one launch (start us, length us, event | category | flops | bytes accessed | tf_op | source)
XLA Modules:
  0.0 101.1 jit_solution(11559158989936609169)
XLA Ops:
  0.6 99.0 %shard_map.67 = (bf16[16,6144]{1,0:T(8,128)(2,1)S(1)}, f32[384,2,384]{2,1,0:T(2,128)S(1)}, f32[384,2,128]{2,1,0:T(2,128)S(1)}) custom-call(bf16[256,6144]{1,0:T(8,128)(2,1)} %x_hbm.1, bf16[384,2,384]{2,1,0:T(2,128)(2,1)} %wq_raw_hbm.1, bf16[384,2,128]{2,1,0:T(2,128)(2,1)} %wo_raw_hbm.1, bf16[256,6144]{1,0:T(8,128)(2,1)} %up_hbm.1), custom_call_target="tpu_custom_call" | custom-call | flops 10000000000 | bytes 10000000 | tf_op jit(solution)/shard_map/pallas_call | solution.py:704
  99.7 1.2 %shard_map.68 = (bf16[16,6144]{1,0:T(8,128)(2,1)}, f32[384,2,384]{2,1,0:T(2,128)}, f32[384,2,128]{2,1,0:T(2,128)}) custom-call(bf16[16,6144]{1,0:T(8,128)(2,1)S(1)} %get-tuple-element.6.refs_0_, f32[384,2,384]{2,1,0:T(2,128)S(1)} %get-tuple-element.7.refs_1_, f32[384,2,128]{2,1,0:T(2,128)S(1)} %get-tuple-element.8.refs_2_), custom_call_target="tpu_custom_call" | custom-call | tf_op jit(solution)/shard_map/pallas_call | solution.py:657

commit v4 on v3

--- a/solution.py
+++ b/solution.py
@@ -20,7 +20,7 @@
 QW = 3 * HEAD
 N_CHIPS = 8
 N_DP = 16
-GROUPS = 4
+GROUPS = 8
 N_MESSAGES = 200
 SLOT_ORDER = (0, 3, 1, 4, 7, 5, 2, 6)
 
@@ -115,9 +115,11 @@
         pltpu.make_async_copy(wo_raw_hbm, wo_raw, local_sem.at[3]),
         pltpu.make_async_copy(up_hbm, up.at[0], local_sem.at[4]),
     ]
-    for n in (2, 3, 0, 1):
-        loads[n].start()
+    loads[2].start()
+    loads[3].start()
     loads[2].wait()
+    loads[0].start()
+    loads[1].start()
     for h in range(2):
         wq_own[h] = wq_raw[:, h, :]
     loads[3].wait()
@@ -453,10 +455,9 @@
                 rows_other[:, lanes] = part.T.astype(BF16)
 
     def gn_group(g):
-        for slot in (2 * g, 2 * g + 1):
-            share_msgs[SLOT_ORDER.index(slot)].wait_recv()
-            part = mm_nt(rows[...], wq[slot].reshape(CHIP_D, 2 * QW)).astype(BF16)
-            gn[slot] = part.reshape(2, 128, CHIP_D)
+        share_msgs[SLOT_ORDER.index(g)].wait_recv()
+        part = mm_nt(rows[...], wq[g].reshape(CHIP_D, 2 * QW)).astype(BF16)
+        gn[g] = part.reshape(2, 128, CHIP_D)
         gn_step0(g)
 
     def z_rows(dz):
@@ -467,28 +468,23 @@
 
     def gn_step0(g):
         for n, (target, _) in enumerate(directions):
-            zm_msgs[g, 0, n] = send(gn.at[2 * g + n, :, z_rows(4)], zr0.at[n, g], target)
+            zm_msgs[g, 0, n] = send(gn.at[g, n, z_rows(4)], zr0.at[n, g], target)
 
     def gn_step(g, step):
         for n, (target, sign) in enumerate(directions):
             at = z_rows(sign * (4 - step))
             zm_msgs[g, step - 1, n].wait_recv()
             if step == 1:
-                mine = gn[2 * g + n, :, at, :].astype(F32)
-                gn[2 * g + n, :, at, :] = (mine + zr0[n, g].astype(F32)).astype(BF16)
+                mine = gn[g, n, at, :].astype(F32)
+                gn[g, n, at, :] = (mine + zr0[n, g].astype(F32)).astype(BF16)
             else:
-                mine = gn[pl.ds(2 * g, 2), :, at, :].astype(F32)
-                mine = mine + zr1[n, g, step - 2].astype(F32)
-                gn[pl.ds(2 * g, 2), :, at, :] = mine.astype(BF16)
-            zm_msgs[g, step, n] = send(
-                gn.at[pl.ds(2 * g, 2), :, at], zr1.at[n, g, step - 1], target
-            )
+                mine = gn[g, :, at, :].astype(F32)
+                gn[g, :, at, :] = (mine + zr1[n, g, step - 2].astype(F32)).astype(BF16)
+            zm_msgs[g, step, n] = send(gn.at[g, :, at], zr1.at[n, g, step - 1], target)
 
     def gn_sum(g, which):
-        at = z_rows(0)
-        pair = pl.ds(2 * g, 2)
-        total = gn[pair, which, at, :].astype(F32)
-        return total + zr1[0, g, 2, :, which].astype(F32) + zr1[1, g, 2, :, which].astype(F32)
+        total = gn[g, which, z_rows(0), :].astype(F32)
+        return total + zr1[0, g, 2, which].astype(F32) + zr1[1, g, 2, which].astype(F32)
 
     def gn_exchange(g):
         for n in range(2):
@@ -498,9 +494,7 @@
 
     def gn_finish(g):
         zm_msgs[g, "y"].wait_recv()
-        total = gn_sum(g, yh) + yrecv[g].astype(F32)
-        for n in range(2):
-            gnf[:, chip_cols(2 * g + n)] = total[n]
+        gnf[:, chip_cols(g)] = gn_sum(g, yh) + yrecv[g].astype(F32)
 
     def q_units(slot):
         weight_unit(gq, rows_t, nrm, slot)
@@ -533,93 +527,117 @@
 
     g_o.stage1()
     g_o.stage2()
+    forward(0)
     await_up()
+    forward(1)
+    o_units(6)
     project_o(0)
-    forward(0)
-    forward(1)
     g_o.stage3()
-    o_units(6)
+    project_o(4)
+    o_units(1)
+    s_o.send_xb1(1)
+    s_o.send_ya(2)
+    o_units(4)
+    o_units(5)
+    o_units(7)
+    o_units(3)
+    g_o.stage4()
     o_units(2)
-    s_o.send_ya(2)
-    project_o(4)
-    s_o.send_xb1(1)
+    g_o.stage5()
     project_o(3)
-    g_o.stage4()
-    o_units(0)
-    o_units(4)
+    s_o.send_ya(3)
+    s_o.send_ya(1)
     project_o(1)
-    g_o.stage5()
+    s_o.send_ya(0)
+    s_o.send_xb1(0)
     project_o(7)
-    s_o.send_xb1(0)
-    s_o.send_ya(0)
-    o_units(1)
-    o_units(7)
     project_o(5)
+    s_o.step_xa1()
+    s_o.step_xb2(1)
     project_o(2)
-    o_units(5)
-    s_o.send_ya(1)
-    s_o.step_xb2(1)
-    s_o.step_xa1()
-    s_o.send_ya(3)
     project_o(6)
     backward(1)
     share_rows()
     backward(0)
     q_units(6)
     s_q.send_ya(2)
+    await_rows()
     s_q.send_xb1(1)
-    await_rows()
-    gn_group(1)
-    q_units(5)
+    gn_group(6)
+    gn_group(5)
+    gn_group(7)
     gn_group(2)
     q_units(2)
+    s_q.send_xb1(0)
     q_units(7)
-    s_q.send_xb1(0)
+    gn_step(6, 1)
+    gn_group(0)
+    gn_step(5, 1)
+    s_q.send_ya(3)
+    gn_group(3)
+    gn_step(7, 1)
+    gn_step(2, 1)
+    s_o.step_xb2(0)
+    gn_group(4)
+    gn_step(6, 2)
+    s_q.step_xa1()
+    q_units(5)
+    s_q.send_ya(1)
+    gn_step(5, 2)
+    gn_group(1)
+    gn_step(0, 1)
+    s_q.step_xb2(1)
+    gn_step(4, 1)
+    gn_step(3, 1)
+    gn_step(7, 2)
+    q_units(4)
+    q_units(3)
+    s_q.send_ya(0)
+    s_o.step_yb()
+    gn_step(5, 3)
     gn_step(1, 1)
-    s_q.send_ya(1)
-    gn_group(0)
-    gn_step(2, 1)
-    s_q.step_xa1()
-    s_q.send_ya(3)
-    s_q.step_xb2(1)
+    gn_step(2, 2)
+    gn_step(0, 2)
+    q_units(1)
+    gn_step(4, 2)
+    s_o.step_xa2()
+    gn_step(3, 2)
+    s_q.step_xa2()
+    gn_step(6, 3)
     gn_step(1, 2)
+    gn_exchange(5)
+    s_q.step_yb()
+    gn_step(7, 3)
+    gn_step(0, 3)
+    gn_step(4, 3)
+    s_q.step_xb2(0)
+    o_units(0)
+    gn_step(2, 3)
+    gn_step(3, 3)
+    q_units(0)
     s_o.send_own()
-    o_units(3)
-    gn_group(3)
-    gn_step(0, 1)
-    gn_step(2, 2)
-    q_units(4)
-    q_units(0)
-    s_o.step_xa2()
-    q_units(1)
+    gn_exchange(7)
+    gn_step(1, 3)
+    s_o.finish_a(go_out)
+    gn_exchange(4)
+    gn_exchange(6)
+    gn_finish(5)
     s_q.send_own()
-    s_q.send_ya(0)
-    gn_step(3, 1)
-    q_units(3)
-    gn_step(1, 3)
-    gn_step(0, 2)
-    s_o.step_xb2(0)
-    s_o.step_yb()
-    s_q.step_xa2()
-    gn_step(3, 2)
-    s_q.step_yb()
-    gn_step(2, 3)
-    s_q.step_xb2(0)
-    gn_step(0, 3)
-    gn_step(3, 3)
-    s_o.finish_a(go_out)
+    gn_exchange(0)
+    s_o.finish_b(go_out)
+    gn_exchange(3)
     gn_exchange(2)
     gn_exchange(1)
-    gn_exchange(0)
     s_q.finish_a(gq_out)
-    gn_exchange(3)
-    s_o.finish_b(go_out)
-    settle(16)
+    gn_finish(7)
+    gn_finish(4)
+    settle(24)
+    gn_finish(6)
+    s_q.finish_b(gq_out)
+    gn_finish(3)
+    gn_finish(0)
     gn_finish(2)
     gn_finish(1)
-    s_q.finish_b(gq_out)
-    gn_finish(0)
-    gn_finish(3)
     norm_backward()
 
     settle(0)
@@ -688,10 +706,10 @@
         *scatter_buffers(QW),
         *scatter_buffers(HEAD),
         pltpu.VMEM((N_CHIPS, 2, 128, CHIP_D), BF16),
-        pltpu.VMEM((2, GROUPS, 2, 16, CHIP_D), BF16),
-        pltpu.VMEM((2, GROUPS, 3, 2, 2, 16, CHIP_D), BF16),
-        pltpu.VMEM((GROUPS, 2, 16, CHIP_D), BF16),
-        pltpu.VMEM((GROUPS, 2, 16, CHIP_D), BF16),
+        pltpu.VMEM((2, GROUPS, 16, CHIP_D), BF16),
+        pltpu.VMEM((2, GROUPS, 3, 2, 16, CHIP_D), BF16),
+        pltpu.VMEM((GROUPS, 16, CHIP_D), BF16),
+        pltpu.VMEM((GROUPS, 16, CHIP_D), BF16),
         pltpu.VMEM((16, D), F32),
         pltpu.VMEM((16, D), F32),
         pltpu.VMEM((16, 128), F32),

time: 101 us -> 101 us (level)
  no operation moved by 1% of the time
where the time goes in v4:
time: 101 us
  Pallas kernels  99.9 us (99%)
    pallas_call x1, Pallas kernels, per_device(): pl.pallas_call(kernel, out_shape=(pltpu.VMEM((16, D), BF16), pltpu.VMEM((...  98.7 us

profile of v4, /device:TPU:1, one launch (start us, length us, event | category | flops | bytes accessed | tf_op | source)
XLA Modules:
  0.0 100.7 jit_solution(16403980042315406200)
XLA Ops:
  0.6 98.7 %shard_map.67 = (bf16[16,6144]{1,0:T(8,128)(2,1)S(1)}, f32[384,2,384]{2,1,0:T(2,128)S(1)}, f32[384,2,128]{2,1,0:T(2,128)S(1)}) custom-call(bf16[256,6144]{1,0:T(8,128)(2,1)} %x_hbm.1, bf16[384,2,384]{2,1,0:T(2,128)(2,1)} %wq_raw_hbm.1, bf16[384,2,128]{2,1,0:T(2,128)(2,1)} %wo_raw_hbm.1, bf16[256,6144]{1,0:T(8,128)(2,1)} %up_hbm.1), custom_call_target="tpu_custom_call" | custom-call | flops 10000000000 | bytes 10000000 | tf_op jit(solution)/shard_map/pallas_call | solution.py:722
  99.4 1.2 %shard_map.68 = (bf16[16,6144]{1,0:T(8,128)(2,1)}, f32[384,2,384]{2,1,0:T(2,128)}, f32[384,2,128]{2,1,0:T(2,128)}) custom-call(bf16[16,6144]{1,0:T(8,128)(2,1)S(1)} %get-tuple-element.6.refs_0_, f32[384,2,384]{2,1,0:T(2,128)S(1)} %get-tuple-element.7.refs_1_, f32[384,2,128]{2,1,0:T(2,128)S(1)} %get-tuple-element.8.refs_2_), custom_call_target="tpu_custom_call" | custom-call | tf_op jit(solution)/shard_map/pallas_call | solution.py:675

commit v5 on v4

--- a/solution.py
+++ b/solution.py
@@ -121,16 +121,11 @@
     loads[0].start()
     loads[1].start()
     for h in range(2):
-        wq_own[h] = wq_raw[:, h, :]
-    loads[3].wait()
-    for h in range(2):
-        wo_own[h] = wo_raw[:, h, :]
+        wq_own[h, :GATHER_A] = wq_raw[:GATHER_A, h, :]
     own_loads = [
         pltpu.make_async_copy(wq_own.at[core], wq.at[0, core, :, pl.ds(0, QW)], local_sem.at[2]),
         pltpu.make_async_copy(wo_own.at[core], wo.at[0, core], local_sem.at[3]),
     ]
-    for load in own_loads:
-        load.start()
     pl.semaphore_wait(barrier, len(partners))
 
     A = pl.ds(0, GATHER_A)
@@ -141,8 +136,9 @@
     B1 = pl.ds(GATHER_A + GATHER_B0, ROWS - GATHER_A - GATHER_B0)
 
     class Gather:
-        def __init__(self, w, own, load, width):
+        def __init__(self, w, own, load, width, split):
             self.w, self.own, self.load, self.lanes = w, own, load, pl.ds(0, width)
+            self.split = split
 
         def at(self, slot, rows, part=slice(None)):
             return self.w.at[slot, part, rows, self.lanes]
@@ -152,10 +148,12 @@
 
         def stage0(self):
             src = self.own
-            self.swap = send(src.at[other], self.at(0, slice(None), core), sib)
             self.xa_p = [send(src.at[core, A], self.at(3, A, core), xp)]
             self.xa_m = [send(src.at[core, A], self.at(1, A, core), xm)]
+            self.split()
             self.yb = [send(src.at[core, B], self.at(4, B, core), yp)]
+            self.swap = send(src.at[other], self.at(0, slice(None), core), sib)
+            self.load.start()
 
         def stage0b(self):
             self.swap.wait_recv()
@@ -211,9 +209,19 @@
             for m in pending:
                 m.wait_recv()
 
-    g_q = Gather(wq, wq_own, own_loads[0], QW)
-    g_o = Gather(wo, wo_own, own_loads[1], HEAD)
+    def split_q():
+        for h in range(2):
+            wq_own[h, GATHER_A:] = wq_raw[GATHER_A:, h, :]
+
+    def split_o():
+        loads[3].wait()
+        for h in range(2):
+            wo_own[h] = wo_raw[:, h, :]
+
+    g_q = Gather(wq, wq_own, own_loads[0], QW, split_q)
+    g_o = Gather(wo, wo_own, own_loads[1], HEAD, lambda: None)
     g_q.stage0()
+    split_o()
     g_q.stage0b()
 
     loads[0].wait()

time: 101 us -> 99 us (0.980)
  Pallas kernels: 99.9 us -> 98.1 us
    pallas_call x1, Pallas kernels: 98.7 us -> 96.9 us  [per_device(): pl.pallas_call(kernel, out_shape=(pltpu.VMEM((16, D), BF16), pltpu.VMEM((...]
where the time goes in v5:
time: 99 us; the launch traced here: 98.9 us
  Pallas kernels  98.1 us (99%)
    pallas_call x1, Pallas kernels, per_device(): pl.pallas_call(kernel, out_shape=(pltpu.VMEM((16, D), BF16), pltpu.VMEM((...  96.9 us

profile of v5, /device:TPU:1, one launch (start us, length us, event | category | flops | bytes accessed | tf_op | source)
XLA Modules:
  0.0 98.9 jit_solution(10472393770182643095)
XLA Ops:
  0.6 96.9 %shard_map.67 = (bf16[16,6144]{1,0:T(8,128)(2,1)S(1)}, f32[384,2,384]{2,1,0:T(2,128)S(1)}, f32[384,2,128]{2,1,0:T(2,128)S(1)}) custom-call(bf16[256,6144]{1,0:T(8,128)(2,1)} %x_hbm.1, bf16[384,2,384]{2,1,0:T(2,128)(2,1)} %wq_raw_hbm.1, bf16[384,2,128]{2,1,0:T(2,128)(2,1)} %wo_raw_hbm.1, bf16[256,6144]{1,0:T(8,128)(2,1)} %up_hbm.1), custom_call_target="tpu_custom_call" | custom-call | flops 10000000000 | bytes 10000000 | tf_op jit(solution)/shard_map/pallas_call | solution.py:730
  97.5 1.2 %shard_map.68 = (bf16[16,6144]{1,0:T(8,128)(2,1)}, f32[384,2,384]{2,1,0:T(2,128)}, f32[384,2,128]{2,1,0:T(2,128)}) custom-call(bf16[16,6144]{1,0:T(8,128)(2,1)S(1)} %get-tuple-element.6.refs_0_, f32[384,2,384]{2,1,0:T(2,128)S(1)} %get-tuple-element.7.refs_1_, f32[384,2,128]{2,1,0:T(2,128)S(1)} %get-tuple-element.8.refs_2_), custom_call_target="tpu_custom_call" | custom-call | tf_op jit(solution)/shard_map/pallas_call | solution.py:683

commit v6 on v5

--- a/solution.py
+++ b/solution.py
@@ -111,15 +111,21 @@
     loads = [
         pltpu.make_async_copy(x_hbm, xbuf, local_sem.at[0]),
         pltpu.make_async_copy(x_hbm.at[pl.ds(token0, 16)], xrow, local_sem.at[1]),
-        pltpu.make_async_copy(wq_raw_hbm, wq_raw, local_sem.at[2]),
+        pltpu.make_async_copy(
+            wq_raw_hbm.at[pl.ds(0, GATHER_A)], wq_raw.at[pl.ds(0, GATHER_A)], local_sem.at[2]
+        ),
         pltpu.make_async_copy(wo_raw_hbm, wo_raw, local_sem.at[3]),
         pltpu.make_async_copy(up_hbm, up.at[0], local_sem.at[4]),
+        pltpu.make_async_copy(
+            wq_raw_hbm.at[pl.ds(GATHER_A, ROWS - GATHER_A)],
+            wq_raw.at[pl.ds(GATHER_A, ROWS - GATHER_A)],
+            local_sem.at[5],
+        ),
     ]
     loads[2].start()
+    loads[5].start()
     loads[3].start()
     loads[2].wait()
-    loads[0].start()
-    loads[1].start()
     for h in range(2):
         wq_own[h, :GATHER_A] = wq_raw[:GATHER_A, h, :]
     own_loads = [
@@ -210,6 +216,9 @@
                 m.wait_recv()
 
     def split_q():
+        loads[5].wait()
+        loads[0].start()
+        loads[1].start()
         for h in range(2):
             wq_own[h, GATHER_A:] = wq_raw[GATHER_A:, h, :]
 
@@ -721,7 +730,7 @@
         pltpu.VMEM((16, D), F32),
         pltpu.VMEM((16, D), F32),
         pltpu.VMEM((16, 128), F32),
-        pltpu.SemaphoreType.DMA((5,)),
+        pltpu.SemaphoreType.DMA((6,)),
         pltpu.SemaphoreType.DMA((N_MESSAGES,)),
         pltpu.SemaphoreType.DMA((N_MESSAGES,)),
     ]

time: 99 us -> 99 us (level)
  no operation moved by 1% of the time
where the time goes in v6:
time: 99 us; the launch traced here: 98.9 us
  Pallas kernels  98.1 us (99%)
    pallas_call x1, Pallas kernels, per_device(): pl.pallas_call(kernel, out_shape=(pltpu.VMEM((16, D), BF16), pltpu.VMEM((...  96.8 us

profile of v6, /device:TPU:1, one launch (start us, length us, event | category | flops | bytes accessed | tf_op | source)
XLA Modules:
  0.0 98.9 jit_solution(657085187986895457)
XLA Ops:
  0.6 96.8 %shard_map.67 = (bf16[16,6144]{1,0:T(8,128)(2,1)S(1)}, f32[384,2,384]{2,1,0:T(2,128)S(1)}, f32[384,2,128]{2,1,0:T(2,128)S(1)}) custom-call(bf16[256,6144]{1,0:T(8,128)(2,1)} %x_hbm.1, bf16[384,2,384]{2,1,0:T(2,128)(2,1)} %wq_raw_hbm.1, bf16[384,2,128]{2,1,0:T(2,128)(2,1)} %wo_raw_hbm.1, bf16[256,6144]{1,0:T(8,128)(2,1)} %up_hbm.1), custom_call_target="tpu_custom_call" | custom-call | flops 10000000000 | bytes 10000000 | tf_op jit(solution)/shard_map/pallas_call | solution.py:739
  97.5 1.2 %shard_map.68 = (bf16[16,6144]{1,0:T(8,128)(2,1)}, f32[384,2,384]{2,1,0:T(2,128)}, f32[384,2,128]{2,1,0:T(2,128)}) custom-call(bf16[16,6144]{1,0:T(8,128)(2,1)S(1)} %get-tuple-element.6.refs_0_, f32[384,2,384]{2,1,0:T(2,128)S(1)} %get-tuple-element.7.refs_1_, f32[384,2,128]{2,1,0:T(2,128)S(1)} %get-tuple-element.8.refs_2_), custom_call_target="tpu_custom_call" | custom-call | tf_op jit(solution)/shard_map/pallas_call | solution.py:692
